TPU v7x, 128 devices: a whole 4x4x4 slice. The times are simulated.
128 devices in a mesh: gx: 32 (over y, z_hi, x), gy: 4 (over z_lo, core).
Axes of the slice: x: 4, y: 4, z: 4 (z_hi: 2, z_lo: 2; z = z_hi * 2 + z_lo), core: 2. Of those that a mesh axis runs over, the one named last changes fastest.
Arguments:
- permeability: float32 [10, 1024, 512], P(None, 'gx', 'gy'), may hold values from 0.1 to 10
- storage: float32 [10, 1024, 512], P(None, 'gx', 'gy'), may hold values from 0.02 to 0.5
- active_mask: int32 [1024, 512], P('gx', 'gy'), may hold values 0 or 1
- colour: int32 [10, 1024, 512], P(None, 'gx', 'gy'), may hold values from 0 to 1
- restrict_weight: float32 [10, 1024, 512], P(None, 'gx', 'gy'), may hold values from 0.5 to 1.5
- sweeps: int32 [4], replicated, may hold values from 1 to 3, as said below
- aggregate_map: int32 [128, 512], P('gx', 'gy'), may hold values from 0 to 511, as said below
- source_term: float32 [10, 1024, 512], P(None, 'gx', 'gy'), may hold values from -6 to 6
Outputs:
- solution_field: float32 [10, 1024, 512], P(None, 'gx', 'gy')
- final_residual: float32 [10, 1024, 512], P(None, 'gx', 'gy')
Inputs may be any that keep to these rules, and one draw needn't show every extreme that they name: 3 sweeps on at least one level. `aggregate_map`: every aggregate holds some columns in every layer.
All inputs are finite; a program needn't handle non-finite values. No bound on the sum of `active_mask` on one device may be relied on, other than what follows from the above.
Results may differ from a plain program's by a relative error of at most 0.0003.
Values sent between devices are 32-bit elements; how exact they have to be, the bound alone decides.
A program may use at most 192 MiB of HBM per device.

v0:
```python
import jax
import jax.numpy as jnp
from jax import lax
from jax.sharding import PartitionSpec as P

LEVELS = 4


vertical_ratio = 0.5


def padded_2(shard, sides, width):
    for axis, dim in sides:
        size, length = (lax.axis_size(axis), shard.shape[dim])
        up = [(i, (i + 1) % size) for i in range(size - 1)]
        down = [(j, i) for i, j in up]
        last = lax.slice_in_dim(shard, length - width, length, axis=dim)
        initial = lax.slice_in_dim(shard, 0, width, axis=dim)
        before = lax.ppermute(last, axis, up)
        after = lax.ppermute(initial, axis, down)
        shard = jnp.concatenate([before, shard, after], axis=dim)
    return shard


def harmonic(first_value, second_value):
    return 2.0 * first_value * second_value / (first_value + second_value)


def build_level(perm_padded, act_padded, storage, colour):
    centre_perm = perm_padded[:, 1:-1, 1:-1]
    centre_act = act_padded[:, 1:-1, 1:-1]

    def face_term(other_perm, other_act):
        return harmonic(centre_perm, other_perm) * centre_act * other_act

    west_face = face_term(perm_padded[:, :-2, 1:-1], act_padded[:, :-2, 1:-1])
    east_face = face_term(perm_padded[:, 2:, 1:-1], act_padded[:, 2:, 1:-1])
    south_face = face_term(perm_padded[:, 1:-1, :-2], act_padded[:, 1:-1, :-2])
    north_face = face_term(perm_padded[:, 1:-1, 2:], act_padded[:, 1:-1, 2:])
    layered = jnp.pad(centre_perm, ((1, 1), (0, 0), (0, 0)))
    below_face = vertical_ratio * harmonic(centre_perm, layered[:-2]) * centre_act
    above_face = vertical_ratio * harmonic(centre_perm, layered[2:]) * centre_act
    diagonal_sum = (
        storage + west_face + east_face + south_face + north_face + below_face + above_face
    )
    centre = jnp.where(centre_act > 0, diagonal_sum, 1.0)
    return (centre, west_face, east_face, south_face, north_face, below_face, above_face, colour)


def coarsen(level):
    centre, west_face, east_face, south_face, north_face, below_face, above_face, colour = level
    return (
        centre[:, 0::2] + centre[:, 1::2] - 2.0 * east_face[:, 0::2],
        west_face[:, 0::2],
        east_face[:, 1::2],
        south_face[:, 0::2] + south_face[:, 1::2],
        north_face[:, 0::2] + north_face[:, 1::2],
        below_face[:, 0::2] + below_face[:, 1::2],
        above_face[:, 0::2] + above_face[:, 1::2],
        colour[:, 0::2],
    )


def neighbours(level, padded):
    centre, west_face, east_face, south_face, north_face, below_face, above_face, colour = level
    middle = padded[:, 1:-1, 1:-1]
    layered = jnp.pad(middle, ((1, 1), (0, 0), (0, 0)))
    return (
        west_face * padded[:, :-2, 1:-1]
        + east_face * padded[:, 2:, 1:-1]
        + south_face * padded[:, 1:-1, :-2]
        + north_face * padded[:, 1:-1, 2:]
        + below_face * layered[:-2]
        + above_face * layered[2:]
    )


def relax(level, padded, right_side, current, shade):
    updated = (right_side + neighbours(level, padded)) / level[0]
    return jnp.where(level[7] == shade, updated, current)


def one_rim(values):
    return padded_2(values, (("gx", 1), ("gy", 2)), 1)


def residual(level, right_side, current):
    return right_side - (level[0] * current - neighbours(level, one_rim(current)))


def on_device(
    permeability, storage, active_mask, colour, restrict_weight, sweeps, aggregate_map, source_term
):
    layers = permeability.shape[0]
    naggs = lax.axis_size("gx") // 2 * 8 * lax.axis_size("gy")
    act_full = jnp.broadcast_to(active_mask.astype(jnp.float32)[None], permeability.shape)
    rimmed = padded_2(jnp.stack([permeability, act_full]), (("gx", 2), ("gy", 3)), 1)
    level = build_level(rimmed[0], rimmed[1], storage, colour)
    levels = [level]
    for depth in range(LEVELS - 1):
        level = coarsen(level)
        levels.append(level)
    deepest = LEVELS - 1
    flat_map = aggregate_map.reshape(-1)
    one_hot = (flat_map[:, None] == jnp.arange(naggs, dtype=jnp.int32)[None, :]).astype(jnp.float32)
    diag_part = jnp.dot(
        levels[deepest][0].reshape(layers, -1),
        one_hot,
        precision=lax.Precision.HIGHEST,
        preferred_element_type=jnp.float32,
    )
    diag_whole = lax.psum(diag_part, ("gx", "gy"))

    def aggregate_correction(leftover):
        res_part = jnp.dot(
            leftover.reshape(layers, -1),
            one_hot,
            precision=lax.Precision.HIGHEST,
            preferred_element_type=jnp.float32,
        )
        ratio = lax.psum(res_part, ("gx", "gy")) / diag_whole
        spread = jnp.dot(
            ratio, one_hot.T, precision=lax.Precision.HIGHEST, preferred_element_type=jnp.float32
        )
        return spread.reshape(leftover.shape)

    def descend(depth, right_side):
        level = levels[depth]

        def sweep_once(step_index, current):
            current = relax(level, one_rim(current), right_side, current, 0)
            return relax(level, one_rim(current), right_side, current, 1)

        current = lax.fori_loop(0, sweeps[depth], sweep_once, jnp.zeros_like(right_side))
        leftover = residual(level, right_side, current)
        if depth == deepest:
            current = current + aggregate_correction(leftover)
        else:
            if depth == 0:
                leftover = restrict_weight * leftover
            coarse_rhs = leftover[:, 0::2] + leftover[:, 1::2]
            current = current + jnp.repeat(descend(depth + 1, coarse_rhs), 2, axis=1)
        return lax.fori_loop(0, sweeps[depth], sweep_once, current)

    solution_field = descend(0, source_term)
    second_rhs = residual(levels[0], source_term, solution_field)
    solution_field = solution_field + descend(0, second_rhs)
    final_residual = residual(levels[0], source_term, solution_field)
    return (solution_field, final_residual)


def solution(mesh):
    placed = (
        P(None, "gx", "gy"),
        P(None, "gx", "gy"),
        P("gx", "gy"),
        P(None, "gx", "gy"),
        P(None, "gx", "gy"),
        P(),
        P("gx", "gy"),
        P(None, "gx", "gy"),
    )
    return jax.shard_map(
        on_device,
        mesh=mesh,
        in_specs=placed,
        out_specs=(P(None, "gx", "gy"), P(None, "gx", "gy")),
        check_vma=False,
    )
```

profile of v0, /device:TPU:71, one launch (start us, length us, event | category | flops | bytes accessed | tf_op | source)
XLA Modules:
  0.0 1804.7 jit_solution(15160520933773705071)
XLA Ops:
  31.3 85.6 %while.192 = (s32[]{:T(128)}, f32[10,32,128]{2,1,0:T(8,128)S(1)}, s32[]{:T(128)}, s32[10,32,128]{2,1,0:T(8,128)S(1)}, f32[10,32,128]{2,1,0:T(8,128)S(1)}, /*inde...) while((s32[]{:T(128)}, f32[10,32,128]{2,1,0:T(8,128)S(1)}, ...), condition=%wide.region_1.2_spmd, body=%wide.region_0.1_spmd.sunk | while | flops 2058242 | bytes 4482685 | solution.py:134
  53.1 8.1 collective-permute-start.5
  75.5 7.9 collective-permute-start.1
  148.7 40.3 %while.193 = (s32[]{:T(128)}, f32[10,16,128]{2,1,0:T(8,128)S(1)}, s32[]{:T(128)}, s32[10,16,128]{2,1,0:T(8,128)S(1)}, f32[10,16,128]{2,1,0:T(8,128)S(1)}, /*inde...) while((s32[]{:T(128)}, f32[10,16,128]{2,1,0:T(8,128)S(1)}, ...), condition=%wide.region_3.4_spmd, body=%wide.region_2.3_spmd.sunk | while | flops 1034242 | bytes 2334845 | solution.py:134
  169.7 8.1 collective-permute-start.13
  219.7 79.9 %while.194 = (s32[]{:T(128)}, f32[10,8,128]{2,1,0:T(8,128)S(1)}, s32[]{:T(128)}, s32[10,8,128]{2,1,0:T(8,128)S(1)}, f32[10,8,128]{2,1,0:T(8,128)S(1)}, /*index=5...) while((s32[]{:T(128)}, f32[10,8,128]{2,1,0:T(8,128)S(1)}, ...), condition=%wide.region_5.6_spmd, body=%wide.region_4.5_spmd.sunk | while | flops 522242 | bytes 1260925 | solution.py:134
  240.1 8.1 collective-permute-start.21
  330.0 117.8 %while.195 = (s32[]{:T(128)}, f32[10,4,128]{2,1,0:T(4,128)S(1)}, s32[]{:T(128)}, s32[10,4,128]{2,1,0:T(4,128)S(1)}, f32[10,4,128]{2,1,0:T(4,128)S(1)}, /*index=5...) while((s32[]{:T(128)}, f32[10,4,128]{2,1,0:T(4,128)S(1)}, ...), condition=%wide.region_7.8_spmd, body=%wide.region_6.7_spmd.sunk | while | flops 266242 | bytes 723965 | solution.py:134
  350.0 8.1 collective-permute-start.29
  476.8 63.3 %all-reduce.43 = (f32[10,512]{1,0:T(8,128)S(1)}, f32[10,512]{1,0:T(8,128)S(1)}) all-reduce(f32[10,512]{1,0:T(8,128)S(1)} %fusion.452, f32[10,512]{1,0:T(8,128)S(1)} %fusion.451), channel_id=1, replica_groups=mesh['gx'=32,'gy'=4] {'gx','gy'}, use_global_device_ids=true, to_apply=%region_8.9 | all-reduce | flops 10240 | bytes 81920 | tf_op jit(solution)/shard_map/psum | solution.py:121
  540.8 118.2 %while.196 = (s32[]{:T(128)}, f32[10,4,128]{2,1,0:T(4,128)S(1)}, s32[]{:T(128)}, s32[10,4,128]{2,1,0:T(4,128)S(1)}, f32[10,4,128]{2,1,0:T(4,128)S(1)}, /*index=5...) while((s32[]{:T(128)}, f32[10,4,128]{2,1,0:T(4,128)S(1)}, ...), condition=%wide.region_11.12_spmd, body=%wide.region_10.11_spmd.sunk | while | flops 266242 | bytes 723965 | solution.py:143
  561.5 8.2 collective-permute-start.37
  659.1 82.9 %while.197 = (s32[]{:T(128)}, f32[10,8,128]{2,1,0:T(8,128)S(1)}, s32[]{:T(128)}, s32[10,8,128]{2,1,0:T(8,128)S(1)}, f32[10,8,128]{2,1,0:T(8,128)S(1)}, /*index=5...) while((s32[]{:T(128)}, f32[10,8,128]{2,1,0:T(8,128)S(1)}, ...), condition=%wide.region_13.14_spmd, body=%wide.region_12.13_spmd.sunk | while | flops 522242 | bytes 1260925 | solution.py:143
  681.6 7.9 collective-permute-start.45
  702.8 7.9 collective-permute-start.41
  742.1 43.2 %while.198 = (s32[]{:T(128)}, f32[10,16,128]{2,1,0:T(8,128)S(1)}, s32[]{:T(128)}, s32[10,16,128]{2,1,0:T(8,128)S(1)}, f32[10,16,128]{2,1,0:T(8,128)S(1)}, /*inde...) while((s32[]{:T(128)}, f32[10,16,128]{2,1,0:T(8,128)S(1)}, ...), condition=%wide.region_15.16_spmd, body=%wide.region_14.15_spmd.sunk | while | flops 1034242 | bytes 2334845 | solution.py:143
  744.7 7.9 collective-permute-start.49
  765.1 7.9 collective-permute-start.53
  785.4 89.9 %while.199 = (s32[]{:T(128)}, f32[10,32,128]{2,1,0:T(8,128)S(1)}, s32[]{:T(128)}, s32[10,32,128]{2,1,0:T(8,128)S(1)}, f32[10,32,128]{2,1,0:T(8,128)S(1)}, /*inde...) while((s32[]{:T(128)}, f32[10,32,128]{2,1,0:T(8,128)S(1)}, ...), condition=%wide.region_17.18_spmd, body=%wide.region_16.17_spmd.sunk | while | flops 2058242 | bytes 4482685 | solution.py:143
  788.0 7.9 collective-permute-start.57
  809.4 8.0 collective-permute-start.61
  832.5 8.0 collective-permute-start.57
  854.0 8.0 collective-permute-start.61
  907.9 89.9 %while.200 = (s32[]{:T(128)}, f32[10,32,128]{2,1,0:T(8,128)S(1)}, s32[]{:T(128)}, s32[10,32,128]{2,1,0:T(8,128)S(1)}, f32[10,32,128]{2,1,0:T(8,128)S(1)}, /*inde...) while((s32[]{:T(128)}, f32[10,32,128]{2,1,0:T(8,128)S(1)}, ...), condition=%wide.region_19.20_spmd, body=%wide.region_18.19_spmd.sunk | while | flops 2058242 | bytes 4482685 | solution.py:134
  929.7 8.3 collective-permute-start.69
  954.2 7.9 collective-permute-start.65
  975.6 8.0 collective-permute-start.69
  997.8 7.9 collective-permute-start.152
  1032.8 42.1 %while.201 = (s32[]{:T(128)}, f32[10,16,128]{2,1,0:T(8,128)S(1)}, s32[]{:T(128)}, s32[10,16,128]{2,1,0:T(8,128)S(1)}, f32[10,16,128]{2,1,0:T(8,128)S(1)}, /*inde...) while((s32[]{:T(128)}, f32[10,16,128]{2,1,0:T(8,128)S(1)}, ...), condition=%wide.region_21.22_spmd, body=%wide.region_20.21_spmd.sunk | while | flops 1034242 | bytes 2334845 | solution.py:134
  1053.7 8.1 collective-permute-start.77
  1106.4 83.5 %while.202 = (s32[]{:T(128)}, f32[10,8,128]{2,1,0:T(8,128)S(1)}, s32[]{:T(128)}, s32[10,8,128]{2,1,0:T(8,128)S(1)}, f32[10,8,128]{2,1,0:T(8,128)S(1)}, /*index=5...) while((s32[]{:T(128)}, f32[10,8,128]{2,1,0:T(8,128)S(1)}, ...), condition=%wide.region_23.24_spmd, body=%wide.region_22.23_spmd.sunk | while | flops 522242 | bytes 1260925 | solution.py:134
  1126.9 8.1 collective-permute-start.85
  1220.9 123.5 %while.203 = (s32[]{:T(128)}, f32[10,4,128]{2,1,0:T(4,128)S(1)}, s32[]{:T(128)}, s32[10,4,128]{2,1,0:T(4,128)S(1)}, f32[10,4,128]{2,1,0:T(4,128)S(1)}, /*index=5...) while((s32[]{:T(128)}, f32[10,4,128]{2,1,0:T(4,128)S(1)}, ...), condition=%wide.region_25.26_spmd, body=%wide.region_24.25_spmd.sunk | while | flops 266242 | bytes 744473 | solution.py:134
  1241.0 8.1 collective-permute-start.93
  1374.8 62.2 %psum.23 = f32[10,512]{1,0:T(8,128)S(1)} all-reduce(f32[10,512]{1,0:T(8,128)S(1)} %fusion.449), channel_id=1, replica_groups=mesh['gx'=32,'gy'=4] {'gx','gy'}, use_global_device_ids=true, to_apply=%region_26.27 | all-reduce | flops 5120 | bytes 40960 | tf_op jit(solution)/shard_map/psum | solution.py:121
  1437.7 120.1 %while.204 = (s32[]{:T(128)}, f32[10,4,128]{2,1,0:T(4,128)S(1)}, s32[]{:T(128)}, s32[10,4,128]{2,1,0:T(4,128)S(1)}, f32[10,4,128]{2,1,0:T(4,128)S(1)}, /*index=5...) while((s32[]{:T(128)}, f32[10,4,128]{2,1,0:T(4,128)S(1)}, ...), condition=%wide.region_28.29_spmd, body=%wide.region_27.28_spmd.sunk | while | flops 266242 | bytes 723965 | solution.py:143
  1539.0 7.9 collective-permute-start.101
  1557.9 84.8 %while.205 = (s32[]{:T(128)}, f32[10,8,128]{2,1,0:T(8,128)S(1)}, s32[]{:T(128)}, s32[10,8,128]{2,1,0:T(8,128)S(1)}, f32[10,8,128]{2,1,0:T(8,128)S(1)}, /*index=5...) while((s32[]{:T(128)}, f32[10,8,128]{2,1,0:T(8,128)S(1)}, ...), condition=%wide.region_30.31_spmd, body=%wide.region_29.30_spmd.sunk | while | flops 522242 | bytes 1260925 | solution.py:143
  1560.5 7.9 collective-permute-start.105
  1602.5 7.9 collective-permute-start.105
  1642.7 42.4 %while.206 = (s32[]{:T(128)}, f32[10,16,128]{2,1,0:T(8,128)S(1)}, s32[]{:T(128)}, s32[10,16,128]{2,1,0:T(8,128)S(1)}, f32[10,16,128]{2,1,0:T(8,128)S(1)}, /*inde...) while((s32[]{:T(128)}, f32[10,16,128]{2,1,0:T(8,128)S(1)}, ...), condition=%wide.region_32.33_spmd, body=%wide.region_31.32_spmd.sunk | while | flops 1034242 | bytes 2334845 | solution.py:143
  1645.3 7.9 collective-permute-start.113
  1665.9 7.9 collective-permute-start.117
  1685.2 88.0 %while.207 = (s32[]{:T(128)}, f32[10,32,128]{2,1,0:T(8,128)S(1)}, s32[]{:T(128)}, s32[10,32,128]{2,1,0:T(8,128)S(1)}, f32[10,32,128]{2,1,0:T(8,128)S(1)}, /*inde...) while((s32[]{:T(128)}, f32[10,32,128]{2,1,0:T(8,128)S(1)}, ...), condition=%wide.region_34.35_spmd, body=%wide.region_33.34_spmd.sunk | while | flops 2058242 | bytes 4482685 | solution.py:143
  1687.8 7.9 collective-permute-start.121
  1709.2 8.0 collective-permute-start.125
  1731.4 8.0 collective-permute-start.121
  1753.0 8.0 collective-permute-start.125
  (1045 shorter events, 1402.0 us)
Async XLA Ops:
  13.0 11.0 collective-permute-start.130
  31.9 9.8 collective-permute-start
  51.2 10.1 collective-permute-start.4
  73.6 9.8 collective-permute-start
  95.0 9.8 collective-permute-start.4
  116.9 10.0 collective-permute-start.132
  134.6 10.6 collective-permute-start.134
  149.4 9.8 collective-permute-start.8
  167.7 10.1 collective-permute-start.12
  189.1 9.9 collective-permute-start.136
  220.3 9.8 collective-permute-start.16
  238.2 10.1 collective-permute-start.20
  259.1 9.8 collective-permute-start.16
  279.0 9.8 collective-permute-start.20
  299.6 10.0 collective-permute-start.140
  330.6 9.8 collective-permute-start.24
  348.1 10.1 collective-permute-start.28
  368.5 9.8 collective-permute-start.24
  388.1 9.8 collective-permute-start.28
  559.6 10.1 collective-permute-start.36
  679.6 9.9 collective-permute-start.44
  700.9 9.9 collective-permute-start.40
  742.7 9.9 collective-permute-start.48
  763.2 9.9 collective-permute-start.52
  786.1 9.9 collective-permute-start.56
  807.4 9.9 collective-permute-start.60
  830.6 9.9 collective-permute-start.56
  852.1 9.9 collective-permute-start.60
  908.5 9.8 collective-permute-start.64
  927.8 10.2 collective-permute-start.68
  952.2 9.8 collective-permute-start.64
  973.7 9.9 collective-permute-start.68
  997.8 9.9 collective-permute-start.152
  1051.7 10.1 collective-permute-start.76
  1125.0 10.1 collective-permute-start.84
  1239.1 10.1 collective-permute-start.92
  1280.9 9.8 collective-permute-start.92
  1302.9 9.8 collective-permute-start.88
  1517.6 9.8 collective-permute-start.96
  1537.1 9.9 collective-permute-start.100
  1558.5 9.9 collective-permute-start.104
  1600.5 9.9 collective-permute-start.104
  1643.4 9.9 collective-permute-start.112
  1663.9 9.9 collective-permute-start.116
  1685.9 9.9 collective-permute-start.120
  1707.3 9.9 collective-permute-start.124
  1729.5 9.9 collective-permute-start.120
  1751.1 9.9 collective-permute-start.124
  (281 other events, 2520.4 us)
where the time goes:
time: 1810 us; the launch traced here: 1800 us
  starting transfers between devices  1290 us (71%)
  waiting for transfers between devices  279 us (15%)
  blocking collectives  126 us (7%)
  local copies, waits for them, and re-layouts  35.2 us (2%)
  loops' own time  35 us (2%)
  other arithmetic  31.1 us (2%)
    ppermute x150, starting transfers between devices, padded_2(): before = lax.ppermute(last, axis, up)  999 us
    ppermute x150, starting transfers between devices, padded_2(): after = lax.ppermute(initial, axis, down)  295 us
    ppermute x150, waiting for transfers between devices, padded_2(): after = lax.ppermute(initial, axis, down)  152 us
    ppermute x150, waiting for transfers between devices, padded_2(): before = lax.ppermute(last, axis, up)  127 us
    psum x2, blocking collectives, aggregate_correction(): ratio = lax.psum(res_part, ('gx', 'gy')) / diag_whole  126 us
  transfers between devices with their start and end apart: 300, of which 195 were waited for; matrix products, arithmetic and copies ran while one was open for 0% of the time, Pallas kernels for 0%

commit v1 on v0

v1 whole, which is shorter than its diff:
```python
import functools
import jax
import jax.numpy as jnp
from jax import lax
from jax.experimental import pallas as pl
from jax.experimental.pallas import tpu as pltpu
from jax.sharding import PartitionSpec as P

MESH = pl.DeviceIdType.MESH
F32 = jnp.float32
NZ = 10
T2 = 2 * NZ
LEVELS = 4
NAGG = 512
ROWS = (6, 6, 4, 4)
HALO = (8, 16, 12, 12)
OWN = (32, 16, 8, 4)
LIN = (48, 48, 40, 32)
LO = (8, 16, 16, 12)
WS = (0, 0, 4, 0)
REACH = ((1, -1), (1, -1), (1, -1, 2, -2), (1, -1, 2, -2, 3, -3))
SO = 8
ST_ROWS = (48, 32, 24, 24)
ST_OFF = (0, 4, 0, 2)
ES_OFF = (0, 0, 4, 4)
ES_ROWS = (48, 48, 40, 40)
ARR = 24
ZC = 5

X_PARTNERS = ((1, 0), (2, 0), (3, 0))
Y_PARTNERS = ((8, 0), (16, 0), (24, 0))
Z_PARTNERS = ((4, 0), (0, 2), (4, 2))


def pads(buf, rows):
    buf[0] = pltpu.roll(buf[rows], 1, 1)
    buf[rows + 1] = pltpu.roll(buf[1], 7, 1)


def beside(own, other, shift, edge):
    moved, moved_other = pltpu.roll(own, shift, 2), pltpu.roll(other, shift, 2)
    return jnp.where(edge, moved_other, moved), jnp.where(edge, moved, moved_other)


def zshift(buf, row, values, tile, first, last, up):
    base = tile * NZ
    if up:
        tail = values[-1:] if last == NZ else buf[row, base + last : base + last + 1]
        return jnp.concatenate([values[1:], tail], axis=0) if last - first > 1 else tail
    head = values[:1] if first == 0 else buf[row, base + first - 1 : base + first]
    return jnp.concatenate([head, values[:-1]], axis=0) if last - first > 1 else head


def neighbour_sum(cf, src, i, first, last):
    lane = lax.broadcasted_iota(jnp.int32, (last - first, 8, 128), 2)
    span = [slice(t * NZ + first, t * NZ + last) for t in (0, 1)]
    own = [src[i + 1, span[t]] for t in (0, 1)]
    south = beside(own[0], own[1], 1, lane == 0)
    north = beside(own[0], own[1], 127, lane == 127)
    sums = []
    for t in (0, 1):
        acc = cf[i, 0, span[t]] * src[i, span[t]]
        acc += cf[i, 1, span[t]] * src[i + 2, span[t]]
        acc += cf[i, 4, span[t]] * zshift(src, i + 1, own[t], t, first, last, False)
        acc += cf[i, 5, span[t]] * zshift(src, i + 1, own[t], t, first, last, True)
        acc += cf[i, 2, span[t]] * south[t]
        acc += cf[i, 3, span[t]] * north[t]
        sums.append(acc)
    return span, own, sums


def kernel(
    gxn,
    gyn,
    perm,
    stor,
    act,
    colour,
    rweight,
    sweeps,
    amap,
    source,
    sol,
    fres,
    y0,
    yl,
    yr,
    f0,
    rw,
    raw,
    cfs,
    ccs,
    cis,
    cols,
    rps,
    eas,
    ebs,
    ks,
    kw,
    sts,
    lrs,
    ess,
    els,
    cls,
    idx,
    onehot,
    agg,
    ar_keep,
    ar_give,
    ar_core,
    ar_sum,
    ar_in,
    ar_last,
    ratio,
    wlin,
    send,
    recv,
):
    gx, gy = lax.axis_index("gx"), lax.axis_index("gy")
    core = lax.rem(gy, 2)

    def ring(dx, dy):
        return (lax.rem(gx + dx + gxn, gxn), lax.rem(gy + dy + gyn, gyn))

    def flip(dx, dy):
        return (jnp.bitwise_xor(gx, dx), jnp.bitwise_xor(gy, dy))

    counter = [0]

    def sems(n):
        counter[0] += n
        return counter[0] - n

    def copy(src, dst, sem, device):
        return pltpu.make_async_remote_copy(
            src_ref=src, dst_ref=dst, send_sem=send.at[sem], recv_sem=recv.at[sem],
            device_id=device, device_id_type=MESH,
        )

    def start(copies):
        for c in copies:
            c.start()

    def finish(copies):
        for c in copies:
            c.wait()

    barrier = pltpu.get_barrier_semaphore()
    partners = [ring(d, 0) for d in REACH[3]] + [ring(0, 1), ring(0, -1)]
    partners += [flip(*p) for p in X_PARTNERS + Y_PARTNERS + Z_PARTNERS + ((0, 1),)]
    for device in partners:
        pl.semaphore_signal(barrier, inc=1, device_id=device, device_id_type=MESH)

    active = act[...] > 0
    for z in range(NZ):
        y0[z] = jnp.where(active, perm[z], 0.0)
        y0[NZ + z] = jnp.where(active, stor[z], 1.0)
        y0[2 * NZ + z] = colour[z].astype(F32)
        y0[3 * NZ + z] = source[z]
        y0[4 * NZ + z] = rweight[z]
    y0[50, 0:4] = amap[...].astype(F32)
    pl.semaphore_wait(barrier, len(partners))

    s_y = sems(2)
    s_x = sems(2)

    def y_copies(span):
        return [
            copy(y0.at[span], yl.at[span], s_y, ring(0, 1)),
            copy(y0.at[span], yr.at[span], s_y + 1, ring(0, -1)),
        ]

    def x_copies(span, buf, base):
        return [
            copy(buf.at[span, :, 32:40], buf.at[span, :, 0:8], base, ring(1, 0)),
            copy(buf.at[span, :, 8:16], buf.at[span, :, 40:48], base + 1, ring(-1, 0)),
        ]

    def join(k):
        lane = lax.broadcasted_iota(jnp.int32, (NZ, 32, 128), 2)
        part = slice(k * NZ, k * NZ + NZ)
        return y0[part], jnp.where(lane < 64, yr[part], yl[part])

    everything = slice(0, 51)
    start(y_copies(everything))
    for j in range(4):
        agg_id = lax.broadcasted_iota(jnp.int32, (NAGG, 128), 0)
        onehot[j] = (agg_id == amap[j : j + 1, :]).astype(jnp.bfloat16)
    agg[...] = jnp.zeros_like(agg)
    finish(y_copies(everything))
    for k in range(4):
        mine, other = join(k)
        f0[k, 0:NZ, 8:40] = mine
        f0[k, NZ:T2, 8:40] = other
    wlin[...] = jnp.zeros_like(wlin)
    mine, other = join(4)
    wlin[0:NZ, 8:40] = mine
    wlin[NZ:T2, 8:40] = other
    start(x_copies(slice(0, 4), f0, s_x))
    for i in range(6):
        rw[i] = wlin[:, pl.ds(i, 8, stride=6), :]
    mlane = lax.broadcasted_iota(jnp.int32, (4, 128), 1)
    ks[3][100, 8:12] = y0[50, 0:4]
    ks[3][101, 8:12] = jnp.where(mlane < 64, yr[50, 0:4], yl[50, 0:4])
    finish(x_copies(slice(0, 4), f0, s_x))

    ea0 = eas[0]
    for i in range(6):
        ea0[i + 1] = f0[0, :, pl.ds(i, 8, stride=6), :]
    pads(ea0, 6)
    lane = lax.broadcasted_iota(jnp.int32, (NZ, 8, 128), 2)
    sub = lax.broadcasted_iota(jnp.int32, (NZ, 8, 128), 1)
    layer = lax.broadcasted_iota(jnp.int32, (NZ, 8, 128), 0)

    def harmonic(a, b):
        total = a + b
        return jnp.where(total > 0, 2.0 * a * b / jnp.where(total > 0, total, 1.0), 0.0)

    def faces0(i, carry):
        own = [ea0[i + 1, t * NZ : t * NZ + NZ] for t in (0, 1)]
        north = beside(own[0], own[1], 127, lane == 127)
        xg = gx * 32 - 8 + 6 * sub + i
        for t in (0, 1):
            part = slice(t * NZ, t * NZ + NZ)
            west = harmonic(own[t], ea0[i, part])
            yg = gy * 128 + lane
            if t == 1:
                yg = jnp.where(lane < 64, yg + 128, yg - 128)
            raw[0, i, part] = jnp.where((xg == 0) | (xg == 1024), 0.0, west)
            raw[1, i, part] = jnp.where(jnp.bitwise_and(yg, 511) == 511, 0.0, harmonic(own[t], north[t]))
            above = 0.5 * harmonic(own[t], zshift(ea0, i + 1, own[t], t, 0, NZ, True))
            raw[2, i, part] = jnp.where(layer == NZ - 1, 0.0, above)
        return carry

    lax.fori_loop(0, 6, faces0, 0)

    def scaled(l, storage_of, west_of, north_of, above_of, colour_of):
        rows, pad = ROWS[l], eas[l]
        for i in range(rows):
            pad[i + 1] = west_of(i)
        pads(pad, rows)
        for i in range(rows):
            north, above = north_of(i), above_of(i)
            south = beside(north[0:NZ], north[NZ:T2], 1, lane == 0)
            zero = jnp.zeros((1, 8, 128), F32)
            below = [
                jnp.concatenate([zero, above[t * NZ : t * NZ + NZ - 1]], axis=0) for t in (0, 1)
            ]
            storage, shade = storage_of(i), colour_of(i)
            for t in (0, 1):
                part = slice(t * NZ, t * NZ + NZ)
                west, east = pad[i + 1, part], pad[i + 2, part]
                six = (west, east, south[t], north[part], below[t], above[part])
                centre = storage[part] + west + east + south[t] + north[part] + below[t] + above[part]
                inverse = 1.0 / centre
                for k in range(6):
                    cfs[l][i, k, part] = six[k] * inverse
                ccs[l][i, part] = centre
                cis[l][i, part] = inverse
                cols[l][i, part] = shade[part]

    def pick0(k):
        return lambda i: f0[k, :, pl.ds(i, 8, stride=6), :]

    scaled(0, pick0(1), lambda i: raw[0, i], lambda i: raw[1, i], lambda i: raw[2, i], pick0(2))

    for m in range(3):
        even, odd = 2 * m, 2 * m + 1
        five = (
            f0[1, :, pl.ds(even, 8, stride=6), :] + f0[1, :, pl.ds(odd, 8, stride=6), :],
            raw[0, even],
            raw[1, even] + raw[1, odd],
            raw[2, even] + raw[2, odd],
            f0[2, :, pl.ds(even, 8, stride=6), :],
        )
        for k in range(5):
            ks[1][k * T2 : k * T2 + T2, pl.ds(4 + m, 8, stride=3), :] = five[k]
    for l in (2, 3):
        for k in range(5):
            part = slice(k * T2, k * T2 + T2)
            value = ks[l - 1][part, pl.ds(8, 8, stride=2), :]
            if k not in (1, 4):
                value = value + ks[l - 1][part, pl.ds(9, 8, stride=2), :]
            ks[l][part, 8:16] = value

    s_k = [None] + [sems(len(REACH[l])) for l in (1, 2, 3)]
    s_r = [None] + [sems(len(REACH[l])) for l in (1, 2, 3)]
    s_e = [sems(len(REACH[l])) for l in range(4)]
    s_ar = sems(22)

    def spread_copies(l, src, src_at, dst, base):
        n = OWN[l]
        return [
            copy(
                src.at[:, src_at : src_at + n],
                dst.at[:, LO[l] - n * d : LO[l] - n * d + n],
                base + k,
                ring(d, 0),
            )
            for k, d in enumerate(REACH[l])
        ]

    def keep_own(l, src, src_at, dst):
        n = OWN[l]
        dst[:, LO[l] : LO[l] + n] = src[:, src_at : src_at + n]
        if l == 3:
            dst[:, 28:32] = src[:, src_at : src_at + n]

    def k_copies(l):
        return spread_copies(l, ks[l], SO, kw[l], s_k[l])

    def level_coefficients(l):
        keep_own(l, ks[l], SO, kw[l])
        finish(k_copies(l))

        def pick(k):
            return lambda i: kw[l][
                k * T2 : k * T2 + T2, pl.ds(WS[l] + i, 8, stride=ROWS[l]), :
            ]

        scaled(l, pick(0), pick(1), pick(2), pick(3), pick(4))

    def half(l, src, dst, shade):
        def row(i, carry):
            for first in range(0, NZ, ZC):
                span, own, sums = neighbour_sum(cfs[l], src, i, first, first + ZC)
                for t in (0, 1):
                    fresh = rps[l][i, span[t]] + sums[t]
                    dst[i + 1, span[t]] = jnp.where(cols[l][i, span[t]] == shade, fresh, own[t])
            return carry

        lax.fori_loop(0, ROWS[l], row, 0)
        pads(dst, ROWS[l])

    def left_over(l, src, i, first, last):
        span, own, sums = neighbour_sum(cfs[l], src, i, first, last)
        return span, [
            ccs[l][i, span[t]] * (rps[l][i, span[t]] + sums[t] - own[t]) for t in (0, 1)
        ]

    def before(l, lin):
        ea, eb = eas[l], ebs[l]
        for i in range(ROWS[l]):
            scaled_rhs = lin[:, pl.ds(WS[l] + i, 8, stride=ROWS[l]), :] * cis[l][i]
            rps[l][i] = scaled_rhs
            ea[i + 1] = jnp.where(cols[l][i] == 0.0, scaled_rhs, 0.0)
        pads(ea, ROWS[l])
        half(l, ea, eb, 1.0)

        def sweep(j, carry):
            on = j < sweeps[l]
            half(l, eb, ea, jnp.where(on, 0.0, -1.0))
            half(l, ea, eb, jnp.where(on, 1.0, -1.0))
            return carry

        lax.fori_loop(1, 3, sweep, 0)

    def after(l):
        ea, eb = eas[l], ebs[l]

        def sweep(j, carry):
            on = j < sweeps[l]
            half(l, ea, eb, jnp.where(on, 0.0, -1.0))
            half(l, eb, ea, jnp.where(on, 1.0, -1.0))
            return carry

        lax.fori_loop(0, 3, sweep, 0)

    def restrict(l):
        stage, rows = sts[l + 1], ROWS[l] // 2

        for m in range(rows):
            for first in range(0, NZ, ZC):
                total = None
                for i in (2 * m, 2 * m + 1):
                    span, res = left_over(l, ebs[l], i, first, first + ZC)
                    if l == 0:
                        res = [rw[i, span[t]] * res[t] for t in (0, 1)]
                    total = res if total is None else [total[t] + res[t] for t in (0, 1)]
                for t in (0, 1):
                    stage[span[t], pl.ds(ST_OFF[l + 1] + m, 8, stride=rows), :] = total[t]

    def stage_iterate(l):
        for i in range(ROWS[l]):
            ess[l][:, pl.ds(ES_OFF[l] + i, 8, stride=ROWS[l]), :] = ebs[l][i + 1]

    def r_copies(l):
        return spread_copies(l, sts[l], SO, lrs[l], s_r[l])

    def e_copies(l):
        own_at = ES_OFF[l] + HALO[l]
        if l == 0:
            return [
                copy(ess[0].at[:, 32:40], els[0].at[:, 0:8], s_e[0], ring(1, 0)),
                copy(ess[0].at[:, 8:16], els[0].at[:, 40:48], s_e[0] + 1, ring(-1, 0)),
            ]
        return spread_copies(l, ess[l], own_at, els[l], s_e[l])

    def aggregate_ratio(cyc):
        s_a = s_ar + cyc * 11
        for first in range(0, NZ, ZC):
            for i in range(4):
                span, res = left_over(3, ebs[3], i, first, first + ZC)
                wlin[span[0], pl.ds(i, 8, stride=4), :] = res[0]
        for i in range(4):
            wlin[NZ:T2, pl.ds(i, 8, stride=4), :] = ccs[3][i, 0:NZ]
        total = jnp.zeros((3 * ARR, NAGG), F32)
        for i in range(4):
            for z in range(T2):
                agg[z : z + 1] = wlin[z, 12 + i : 13 + i, :]
            value = agg[...]
            high = value.astype(jnp.bfloat16)
            rest = value - high.astype(F32)
            middle = rest.astype(jnp.bfloat16)
            low = (rest - middle.astype(F32)).astype(jnp.bfloat16)
            three = jnp.concatenate([high.astype(F32), middle.astype(F32), low.astype(F32)], axis=0)
            total += lax.dot_general(
                three.astype(jnp.bfloat16), onehot[i], (((1,), (1,)), ((), ())),
                preferred_element_type=F32,
            )
        mine = total[0:ARR] + total[ARR : 2 * ARR] + total[2 * ARR :]
        low_half, high_half = mine[:, 0:256], mine[:, 256:512]
        ar_keep[...] = jnp.where(core == 0, low_half, high_half)
        ar_give[...] = jnp.where(core == 0, high_half, low_half)
        first_copy = copy(ar_give, ar_core.at[cyc], s_a, flip(0, 1))
        first_copy.start()
        stage_iterate(3)
        first_copy.wait()
        ar_sum[0] = ar_keep[...] + ar_core[cyc]
        at = 1
        for stage, group in enumerate((X_PARTNERS, Y_PARTNERS, Z_PARTNERS)):
            copies = [
                copy(ar_sum.at[stage], ar_in.at[cyc, stage, k], s_a + at + k, flip(*p))
                for k, p in enumerate(group)
            ]
            start(copies)
            if stage == 0:
                for l in (3, 2, 1, 0):
                    start(e_copies(l))
                for l in range(4):
                    own_at = ES_OFF[l] + HALO[l]
                    els[l][:, LO[l] : LO[l] + OWN[l]] = ess[l][:, own_at : own_at + OWN[l]]
                els[3][:, 28:32] = ess[3][:, 16:20]
            finish(copies)
            ar_sum[stage + 1] = ar_sum[stage] + ar_in[cyc, stage, 0] + ar_in[cyc, stage, 1] + ar_in[cyc, stage, 2]
            at += 3
        last_copy = copy(ar_sum.at[3], ar_last.at[cyc], s_a + 10, flip(0, 1))
        last_copy.start()
        last_copy.wait()
        mine, other = ar_sum[3], ar_last[cyc]
        low_half = jnp.where(core == 0, mine, other)
        high_half = jnp.where(core == 0, other, mine)
        ratio[0:NZ, 0:256] = low_half[0:NZ] / low_half[NZ:T2]
        ratio[0:NZ, 256:512] = high_half[0:NZ] / high_half[NZ:T2]

    def window_iterate(l):
        finish(e_copies(l))
        for i in range(ROWS[l]):
            now = els[l][:, pl.ds(WS[l] + i, 8, stride=ROWS[l]), :]
            if l < 3:
                at = HALO[l + 1] - HALO[l] // 2 + i // 2
                now = now + cls[l + 1][:, pl.ds(at, 8, stride=ROWS[l] // 2), :]
            eas[l][i + 1] = now

    def add_aggregates():
        def row(i, carry):
            for t in (0, 1):
                where = idx[i, t]
                place, block = jnp.bitwise_and(where, 127), jnp.right_shift(where, 7)
                for z in range(NZ):
                    value = jnp.zeros((8, 128), F32)
                    for k in range(4):
                        table = jnp.broadcast_to(
                            ratio[z : z + 1, 128 * k : 128 * k + 128], (8, 128)
                        )
                        found = jnp.take_along_axis(table, place, axis=1)
                        value = jnp.where(block == k, found, value)
                    eas[3][i + 1, t * NZ + z] += value
            return carry

        lax.fori_loop(0, 4, row, 0)

    def cycle(cyc, carry):
        first = cyc == 0
        for l in range(4):
            before(l, f0.at[3] if l == 0 else lrs[l])
            if l < 3:
                restrict(l)
                start(r_copies(l + 1))

                @pl.when(first)
                def _():
                    if l == 0:
                        start(k_copies(1))
                    level_coefficients(l + 1)
                    if l + 1 < 3:
                        start(k_copies(l + 2))
                    else:
                        for i in range(4):
                            for t in (0, 1):
                                found = kw[3][100 + t, pl.ds(i, 8, stride=4), :]
                                idx[i, t] = found.astype(jnp.int32)

                stage_iterate(l)
                keep_own(l + 1, sts[l + 1], SO, lrs[l + 1])
                finish(r_copies(l + 1))
        aggregate_ratio(cyc)
        for l in (3, 2, 1, 0):
            window_iterate(l)
            if l == 3:
                add_aggregates()
            pads(eas[l], ROWS[l])
            after(l)
            if l > 0:
                for i in range(ROWS[l]):
                    cls[l][:, pl.ds(i, 8, stride=ROWS[l]), :] = eas[l][i + 1]

        for i in range(6):
            wlin[0:NZ, pl.ds(i, 8, stride=6), :] = eas[0][i + 1, 0:NZ]
        added = wlin[0:NZ, 8:40]

        @pl.when(first)
        def _():
            sol[...] = added

        @pl.when(jnp.logical_not(first))
        def _():
            sol[...] += added

        for i in range(6):
            for z in range(0, NZ, ZC):
                span, res = left_over(0, eas[0], i, z, z + ZC)
                wlin[span[0], pl.ds(i, 8, stride=6), :] = res[0]
        leftover = wlin[0:NZ, 8:40]

        @pl.when(first)
        def _():
            part = slice(3 * NZ, 4 * NZ)
            y0[part] = leftover
            start(y_copies(part))
            finish(y_copies(part))
            mine, other = join(3)
            f0[3, 0:NZ, 8:40] = mine
            f0[3, NZ:T2, 8:40] = other
            start(x_copies(slice(3, 4), f0, s_x))
            finish(x_copies(slice(3, 4), f0, s_x))

        @pl.when(jnp.logical_not(first))
        def _():
            fres[...] = leftover

        return carry

    lax.fori_loop(0, 2, cycle, 0)


def on_device(gxn, gyn, perm, stor, act, colour, rweight, sweeps, amap, source):
    def vm(*shape, dtype=F32):
        return pltpu.VMEM(shape, dtype)

    levels = range(LEVELS)
    scratch = [
        vm(51, 32, 128),
        vm(51, 32, 128),
        vm(51, 32, 128),
        vm(4, T2, 48, 128),
        vm(6, T2, 8, 128),
        vm(3, 6, T2, 8, 128),
        [vm(ROWS[l], 6, T2, 8, 128) for l in levels],
        [vm(ROWS[l], T2, 8, 128) for l in levels],
        [vm(ROWS[l], T2, 8, 128) for l in levels],
        [vm(ROWS[l], T2, 8, 128) for l in levels],
        [vm(ROWS[l], T2, 8, 128) for l in levels],
        [vm(ROWS[l] + 2, T2, 8, 128) for l in levels],
        [vm(ROWS[l] + 2, T2, 8, 128) for l in levels],
        [vm(102 if l == 3 else 100, ST_ROWS[l], 128) for l in levels],
        [vm(102 if l == 3 else 100, LIN[l], 128) for l in levels],
        [vm(T2, ST_ROWS[l], 128) for l in levels],
        [vm(T2, LIN[l], 128) for l in levels],
        [vm(T2, ES_ROWS[l], 128) for l in levels],
        [vm(T2, LIN[l], 128) for l in levels],
        [vm(T2, 8 * ROWS[l], 128) for l in levels],
        vm(4, 2, 8, 128, dtype=jnp.int32),
        vm(4, NAGG, 128, dtype=jnp.bfloat16),
        vm(ARR, 128),
        vm(ARR, 256),
        vm(ARR, 256),
        vm(2, ARR, 256),
        vm(4, ARR, 256),
        vm(2, 3, 3, ARR, 256),
        vm(2, ARR, 256),
        vm(16, NAGG),
        vm(T2, 48, 128),
        pltpu.SemaphoreType.DMA((64,)),
        pltpu.SemaphoreType.DMA((64,)),
    ]
    vmem = pl.BlockSpec(memory_space=pltpu.VMEM)
    smem = pl.BlockSpec(memory_space=pltpu.SMEM)
    out = jax.ShapeDtypeStruct(perm.shape, F32)
    return pl.pallas_call(
        functools.partial(kernel, gxn, gyn),
        out_shape=(out, out),
        in_specs=[vmem, vmem, vmem, vmem, vmem, smem, vmem, vmem],
        out_specs=(vmem, vmem),
        scratch_shapes=scratch,
        compiler_params=pltpu.CompilerParams(
            collective_id=0, has_side_effects=True, vmem_limit_bytes=60 * 2**20
        ),
    )(perm, stor, act, colour, rweight, sweeps, amap, source)


def solution(mesh):
    field = P(None, "gx", "gy")
    column = P("gx", "gy")
    return jax.shard_map(
        functools.partial(on_device, mesh.shape["gx"], mesh.shape["gy"]),
        mesh=mesh,
        in_specs=(field, field, column, field, field, P(), column, field),
        out_specs=(field, field),
        check_vma=False,
    )
```

time: 1810 us -> 269 us (0.15)
  the two profiles are of different devices: /device:TPU:71 before, /device:TPU:1 now
where the time goes in v1:
time: 269 us; the launch traced here: 268 us
  Pallas kernels  265 us (99%)
    pallas_call x1, Pallas kernels, on_device(): pl.pallas_call(functools.partial(kernel, gxn, gyn), out_shape=(out, out),...  265 us

profile of v1, /device:TPU:1, one launch (start us, length us, event | category | flops | bytes accessed | tf_op | source)
XLA Modules:
  0.0 268.1 jit_solution(7630151222860445161)
XLA Ops:
  0.6 265.1 %shard_map.95 = (f32[10,32,128]{2,1,0:T(8,128)}, f32[10,32,128]{2,1,0:T(8,128)}) custom-call(f32[10,32,128]{2,1,0:T(8,128)} %perm.1, f32[10,32,128]{2,1,0:T(8,128)} %stor.1, s32[32,128]{1,0:T(8,128)} %act.1, s32[10,32,128]{2,1,0:T(8,128)} %colour.1, f32[10,32,128]{2,1,0:T(8,128)} %rweight.1, s32[4]{0:T(128)} %sweeps.1, s32[4,128]{1,0:T(4,128)} %amap.1, ...), custom_call_target="tpu_custom_call" | custom-call | tf_op jit(solution)/shard_map/pallas_call | solution.py:600
  265.8 0.0 copy-start
  265.8 1.6 copy.12
  267.4 0.0 copy-done
  267.4 0.7 copy.13
Async XLA Ops:
  265.8 1.6 copy-start

commit v2 on v1

--- a/solution.py
+++ b/solution.py
@@ -18,14 +18,31 @@
 LIN = (48, 48, 40, 32)
 LO = (8, 16, 16, 12)
 WS = (0, 0, 4, 0)
-REACH = ((1, -1), (1, -1), (1, -1, 2, -2), (1, -1, 2, -2, 3, -3))
+NEAR = (
+    (),
+    ((1, 8, 16, 8, 16), (-1, 0, 8, 32, 40)),
+    ((1, 0, 8, 8, 16), (-1, 0, 8, 24, 32)),
+    ((1, 0, 4, 8, 12), (-1, 0, 4, 16, 20), (2, 0, 4, 4, 8), (-2, 0, 4, 20, 24)),
+)
+FAR = (
+    (),
+    ((1, 4, 8, 4, 8), (-1, 8, 12, 40, 44)),
+    ((2, 4, 8, 4, 8), (-2, 0, 4, 32, 36)),
+    ((3, 0, 4, 0, 4), (-3, 0, 4, 24, 28)),
+)
+ITERATE = (
+    ((1, 24, 32, 0, 8), (-1, 0, 8, 40, 48)),
+    ((1, 4, 16, 4, 16), (-1, 0, 12, 32, 44)),
+    NEAR[2] + FAR[2],
+    NEAR[3] + FAR[3],
+)
 SO = 8
 ST_ROWS = (48, 32, 24, 24)
 ST_OFF = (0, 4, 0, 2)
 ES_OFF = (0, 0, 4, 4)
 ES_ROWS = (48, 48, 40, 40)
 ARR = 24
-ZC = 5
+ZC = 2
 
 X_PARTNERS = ((1, 0), (2, 0), (3, 0))
 Y_PARTNERS = ((8, 0), (16, 0), (24, 0))
@@ -83,8 +100,8 @@
     sol,
     fres,
     y0,
-    yl,
-    yr,
+    yp,
+    yn,
     f0,
     rw,
     raw,
@@ -97,8 +114,10 @@
     ebs,
     ks,
     kw,
+    kf,
     sts,
     lrs,
+    lrf,
     ess,
     els,
     cls,
@@ -146,7 +165,7 @@
             c.wait()
 
     barrier = pltpu.get_barrier_semaphore()
-    partners = [ring(d, 0) for d in REACH[3]] + [ring(0, 1), ring(0, -1)]
+    partners = [ring(d, 0) for d in (1, -1, 2, -2, 3, -3)] + [ring(0, 1), ring(0, -1)]
     partners += [flip(*p) for p in X_PARTNERS + Y_PARTNERS + Z_PARTNERS + ((0, 1),)]
     for device in partners:
         pl.semaphore_signal(barrier, inc=1, device_id=device, device_id_type=MESH)
@@ -158,17 +177,50 @@
         y0[2 * NZ + z] = colour[z].astype(F32)
         y0[3 * NZ + z] = source[z]
         y0[4 * NZ + z] = rweight[z]
-    y0[50, 0:4] = amap[...].astype(F32)
-    pl.semaphore_wait(barrier, len(partners))
+    own_map = amap[...].astype(F32)
 
     s_y = sems(2)
     s_x = sems(2)
 
-    def y_copies(span):
-        return [
-            copy(y0.at[span], yl.at[span], s_y, ring(0, 1)),
-            copy(y0.at[span], yr.at[span], s_y + 1, ring(0, -1)),
-        ]
+    lane10 = lax.broadcasted_iota(jnp.int32, (NZ, 16, 128), 2)
+
+    def pack(k):
+        part = slice(k * NZ, k * NZ + NZ)
+        upper, lower = y0[part, 0:16], y0[part, 16:32]
+        yp[0, part] = jnp.where(lane10 < 64, pltpu.roll(upper, 64, 2), lower)
+        yp[1, part] = jnp.where(lane10 < 64, upper, pltpu.roll(lower, 64, 2))
+
+    def y_exchange(span, between):
+        right = copy(yp.at[0, span], yn.at[0, span], s_y, ring(0, 1))
+        left = copy(yp.at[1, span], yn.at[1, span], s_y + 1, ring(0, -1))
+
+        @pl.when(gy < gyn - 1)
+        def _():
+            right.start()
+
+        @pl.when(gy > 0)
+        def _():
+            left.start()
+
+        @pl.when(gy == 0)
+        def _():
+            yn[0, span] = yp[0, span]
+
+        @pl.when(gy == gyn - 1)
+        def _():
+            yn[1, span] = yp[1, span]
+
+        between()
+
+        @pl.when(gy < gyn - 1)
+        def _():
+            right.wait_send()
+            left.wait_recv()
+
+        @pl.when(gy > 0)
+        def _():
+            left.wait_send()
+            right.wait_recv()
 
     def x_copies(span, buf, base):
         return [
@@ -177,31 +229,51 @@
         ]
 
     def join(k):
-        lane = lax.broadcasted_iota(jnp.int32, (NZ, 32, 128), 2)
         part = slice(k * NZ, k * NZ + NZ)
-        return y0[part], jnp.where(lane < 64, yr[part], yl[part])
-
-    everything = slice(0, 51)
-    start(y_copies(everything))
-    for j in range(4):
-        agg_id = lax.broadcasted_iota(jnp.int32, (NAGG, 128), 0)
-        onehot[j] = (agg_id == amap[j : j + 1, :]).astype(jnp.bfloat16)
-    agg[...] = jnp.zeros_like(agg)
-    finish(y_copies(everything))
+        right, left = yn[1, part], yn[0, part]
+        upper = jnp.where(lane10 < 64, right, pltpu.roll(left, 64, 2))
+        lower = jnp.where(lane10 < 64, pltpu.roll(right, 64, 2), left)
+        return upper, lower
+
+    def fill_beside():
+        for j in range(4):
+            agg_id = lax.broadcasted_iota(jnp.int32, (NAGG, 128), 0)
+            onehot[j] = (agg_id == amap[j : j + 1, :]).astype(jnp.bfloat16)
+        agg[...] = jnp.zeros_like(agg)
+        wlin[...] = jnp.zeros_like(wlin)
+        for l in (1, 2, 3):
+            lrs[l][...] = jnp.zeros_like(lrs[l])
+            els[l][...] = jnp.zeros_like(els[l])
+        for _, _, _, at, end in FAR[1] + ((0, 0, 0, 0, 4), (0, 0, 0, 44, 48)):
+            kw[1][:, at:end] = jnp.ones((100, end - at, 128), F32)
+        for l in (2, 3):
+            for _, _, _, at, end in FAR[l]:
+                kw[l][0:100, at:end] = jnp.ones((100, end - at, 128), F32)
+        for _, _, _, at, end in FAR[3]:
+            kw[3][100:102, at:end] = jnp.zeros((2, end - at, 128), F32)
+        for k in range(4):
+            f0[k, 0:NZ, 8:40] = y0[k * NZ : k * NZ + NZ]
+        wlin[0:NZ, 8:40] = y0[4 * NZ : 5 * NZ]
+
+    for k in range(5):
+        pack(k)
+    yp[0, 50, 0:4] = own_map
+    yp[1, 50, 0:4] = own_map
+    pl.semaphore_wait(barrier, len(partners))
+    y_exchange(slice(0, 51), fill_beside)
     for k in range(4):
-        mine, other = join(k)
-        f0[k, 0:NZ, 8:40] = mine
-        f0[k, NZ:T2, 8:40] = other
-    wlin[...] = jnp.zeros_like(wlin)
-    mine, other = join(4)
-    wlin[0:NZ, 8:40] = mine
-    wlin[NZ:T2, 8:40] = other
+        upper, lower = join(k)
+        f0[k, NZ:T2, 8:24] = upper
+        f0[k, NZ:T2, 24:40] = lower
+    upper, lower = join(4)
+    wlin[NZ:T2, 8:24] = upper
+    wlin[NZ:T2, 24:40] = lower
     start(x_copies(slice(0, 4), f0, s_x))
     for i in range(6):
         rw[i] = wlin[:, pl.ds(i, 8, stride=6), :]
     mlane = lax.broadcasted_iota(jnp.int32, (4, 128), 1)
-    ks[3][100, 8:12] = y0[50, 0:4]
-    ks[3][101, 8:12] = jnp.where(mlane < 64, yr[50, 0:4], yl[50, 0:4])
+    ks[3][100, 8:12] = own_map
+    ks[3][101, 8:12] = jnp.where(mlane < 64, yn[1, 50, 0:4], yn[0, 50, 0:4])
     finish(x_copies(slice(0, 4), f0, s_x))
 
     ea0 = eas[0]
@@ -216,7 +288,7 @@
         total = a + b
         return jnp.where(total > 0, 2.0 * a * b / jnp.where(total > 0, total, 1.0), 0.0)
 
-    def faces0(i, carry):
+    for i in range(6):
         own = [ea0[i + 1, t * NZ : t * NZ + NZ] for t in (0, 1)]
         north = beside(own[0], own[1], 127, lane == 127)
         xg = gx * 32 - 8 + 6 * sub + i
@@ -230,9 +302,6 @@
             raw[1, i, part] = jnp.where(jnp.bitwise_and(yg, 511) == 511, 0.0, harmonic(own[t], north[t]))
             above = 0.5 * harmonic(own[t], zshift(ea0, i + 1, own[t], t, 0, NZ, True))
             raw[2, i, part] = jnp.where(layer == NZ - 1, 0.0, above)
-        return carry
-
-    lax.fori_loop(0, 6, faces0, 0)
 
     def scaled(l, storage_of, west_of, north_of, above_of, colour_of):
         rows, pad = ROWS[l], eas[l]
@@ -283,22 +352,30 @@
                 value = value + ks[l - 1][part, pl.ds(9, 8, stride=2), :]
             ks[l][part, 8:16] = value
 
-    s_k = [None] + [sems(len(REACH[l])) for l in (1, 2, 3)]
-    s_r = [None] + [sems(len(REACH[l])) for l in (1, 2, 3)]
-    s_e = [sems(len(REACH[l])) for l in range(4)]
+    s_kn = [sems(len(NEAR[l])) for l in range(4)]
+    s_kf = [sems(len(FAR[l])) for l in range(4)]
+    s_rn = [sems(len(NEAR[l])) for l in range(4)]
+    s_rf = [sems(len(FAR[l])) for l in range(4)]
+    s_e = [sems(len(ITERATE[l])) for l in range(4)]
     s_ar = sems(22)
 
-    def spread_copies(l, src, src_at, dst, base):
-        n = OWN[l]
+    def near_copies(l, src, own_at, dst, base, table):
+        return [
+            copy(src.at[:, own_at + a : own_at + b], dst.at[:, c:d], base + k, ring(right, 0))
+            for k, (right, a, b, c, d) in enumerate(table)
+        ]
+
+    def far_copies(l, src, dst, base):
         return [
             copy(
-                src.at[:, src_at : src_at + n],
-                dst.at[:, LO[l] - n * d : LO[l] - n * d + n],
-                base + k,
-                ring(d, 0),
+                src.at[:, SO + a : SO + b], dst.at[k, :, c % 8 : c % 8 + 4], base + k, ring(right, 0)
             )
-            for k, d in enumerate(REACH[l])
+            for k, (right, a, b, c, d) in enumerate(FAR[l])
         ]
+
+    def merge_far(l, far, dst):
+        for k, (right, a, b, c, d) in enumerate(FAR[l]):
+            dst[:, c:d] = far[k, :, c % 8 : c % 8 + 4]
 
     def keep_own(l, src, src_at, dst):
         n = OWN[l]
@@ -306,13 +383,16 @@
         if l == 3:
             dst[:, 28:32] = src[:, src_at : src_at + n]
 
-    def k_copies(l):
-        return spread_copies(l, ks[l], SO, kw[l], s_k[l])
+    def kn_copies(l):
+        return near_copies(l, ks[l], SO, kw[l], s_kn[l], NEAR[l])
+
+    def kf_copies(l):
+        return far_copies(l, ks[l], kf[l], s_kf[l])
+
+    def rf_copies(l):
+        return far_copies(l, sts[l], lrf[l], s_rf[l])
 
     def level_coefficients(l):
-        keep_own(l, ks[l], SO, kw[l])
-        finish(k_copies(l))
-
         def pick(k):
             return lambda i: kw[l][
                 k * T2 : k * T2 + T2, pl.ds(WS[l] + i, 8, stride=ROWS[l]), :
@@ -321,15 +401,12 @@
         scaled(l, pick(0), pick(1), pick(2), pick(3), pick(4))
 
     def half(l, src, dst, shade):
-        def row(i, carry):
+        for i in range(ROWS[l]):
             for first in range(0, NZ, ZC):
                 span, own, sums = neighbour_sum(cfs[l], src, i, first, first + ZC)
                 for t in (0, 1):
                     fresh = rps[l][i, span[t]] + sums[t]
                     dst[i + 1, span[t]] = jnp.where(cols[l][i, span[t]] == shade, fresh, own[t])
-            return carry
-
-        lax.fori_loop(0, ROWS[l], row, 0)
         pads(dst, ROWS[l])
 
     def left_over(l, src, i, first, last):
@@ -384,17 +461,11 @@
         for i in range(ROWS[l]):
             ess[l][:, pl.ds(ES_OFF[l] + i, 8, stride=ROWS[l]), :] = ebs[l][i + 1]
 
-    def r_copies(l):
-        return spread_copies(l, sts[l], SO, lrs[l], s_r[l])
+    def rn_copies(l):
+        return near_copies(l, sts[l], SO, lrs[l], s_rn[l], NEAR[l])
 
     def e_copies(l):
-        own_at = ES_OFF[l] + HALO[l]
-        if l == 0:
-            return [
-                copy(ess[0].at[:, 32:40], els[0].at[:, 0:8], s_e[0], ring(1, 0)),
-                copy(ess[0].at[:, 8:16], els[0].at[:, 40:48], s_e[0] + 1, ring(-1, 0)),
-            ]
-        return spread_copies(l, ess[l], own_at, els[l], s_e[l])
+        return near_copies(l, ess[l], ES_OFF[l] + HALO[l], els[l], s_e[l], ITERATE[l])
 
     def aggregate_ratio(cyc):
         s_a = s_ar + cyc * 11
@@ -435,12 +506,8 @@
             ]
             start(copies)
             if stage == 0:
-                for l in (3, 2, 1, 0):
-                    start(e_copies(l))
-                for l in range(4):
-                    own_at = ES_OFF[l] + HALO[l]
-                    els[l][:, LO[l] : LO[l] + OWN[l]] = ess[l][:, own_at : own_at + OWN[l]]
-                els[3][:, 28:32] = ess[3][:, 16:20]
+                start(e_copies(3))
+                keep_own(3, ess[3], 16, els[3])
             finish(copies)
             ar_sum[stage + 1] = ar_sum[stage] + ar_in[cyc, stage, 0] + ar_in[cyc, stage, 1] + ar_in[cyc, stage, 2]
             at += 3
@@ -453,7 +520,19 @@
         ratio[0:NZ, 0:256] = low_half[0:NZ] / low_half[NZ:T2]
         ratio[0:NZ, 256:512] = high_half[0:NZ] / high_half[NZ:T2]
 
-    def window_iterate(l):
+    def window_iterate(l, first):
+        if l > 0:
+
+            @pl.when(first)
+            def _():
+                finish(kf_copies(l))
+                merge_far(l, kf[l], kw[l])
+                level_coefficients(l)
+
+            finish(rf_copies(l))
+            merge_far(l, lrf[l], lrs[l])
+            for i in range(ROWS[l]):
+                rps[l][i] = lrs[l][:, pl.ds(WS[l] + i, 8, stride=ROWS[l]), :] * cis[l][i]
         finish(e_copies(l))
         for i in range(ROWS[l]):
             now = els[l][:, pl.ds(WS[l] + i, 8, stride=ROWS[l]), :]
@@ -480,34 +559,47 @@
 
         lax.fori_loop(0, 4, row, 0)
 
+    for l in (1, 2, 3):
+        start(kn_copies(l))
+
     def cycle(cyc, carry):
         first = cyc == 0
         for l in range(4):
             before(l, f0.at[3] if l == 0 else lrs[l])
             if l < 3:
                 restrict(l)
-                start(r_copies(l + 1))
+                start(rn_copies(l + 1))
+                stage_iterate(l)
+                if l > 0:
+                    start(rf_copies(l))
+                start(e_copies(l))
+                if l == 2:
+                    start(rf_copies(3))
+                keep_own(l, ess[l], ES_OFF[l] + HALO[l], els[l])
+                keep_own(l + 1, sts[l + 1], SO, lrs[l + 1])
 
                 @pl.when(first)
                 def _():
-                    if l == 0:
-                        start(k_copies(1))
+                    if l == 2:
+                        for k in (3, 2, 1):
+                            start(kf_copies(k))
+                    keep_own(l + 1, ks[l + 1], SO, kw[l + 1])
+                    finish(kn_copies(l + 1))
                     level_coefficients(l + 1)
-                    if l + 1 < 3:
-                        start(k_copies(l + 2))
-                    else:
-                        for i in range(4):
-                            for t in (0, 1):
-                                found = kw[3][100 + t, pl.ds(i, 8, stride=4), :]
-                                idx[i, t] = found.astype(jnp.int32)
-
-                stage_iterate(l)
-                keep_own(l + 1, sts[l + 1], SO, lrs[l + 1])
-                finish(r_copies(l + 1))
+
+                finish(rn_copies(l + 1))
         aggregate_ratio(cyc)
         for l in (3, 2, 1, 0):
-            window_iterate(l)
+            window_iterate(l, first)
             if l == 3:
+
+                @pl.when(first)
+                def _():
+                    for i in range(4):
+                        for t in (0, 1):
+                            found = kw[3][100 + t, pl.ds(i, 8, stride=4), :]
+                            idx[i, t] = found.astype(jnp.int32)
+
                 add_aggregates()
             pads(eas[l], ROWS[l])
             after(l)
@@ -537,11 +629,15 @@
         def _():
             part = slice(3 * NZ, 4 * NZ)
             y0[part] = leftover
-            start(y_copies(part))
-            finish(y_copies(part))
-            mine, other = join(3)
-            f0[3, 0:NZ, 8:40] = mine
-            f0[3, NZ:T2, 8:40] = other
+            pack(3)
+
+            def fill_own():
+                f0[3, 0:NZ, 8:40] = y0[part]
+
+            y_exchange(part, fill_own)
+            upper, lower = join(3)
+            f0[3, NZ:T2, 8:24] = upper
+            f0[3, NZ:T2, 24:40] = lower
             start(x_copies(slice(3, 4), f0, s_x))
             finish(x_copies(slice(3, 4), f0, s_x))
 
@@ -560,9 +656,9 @@
 
     levels = range(LEVELS)
     scratch = [
-        vm(51, 32, 128),
-        vm(51, 32, 128),
-        vm(51, 32, 128),
+        vm(50, 32, 128),
+        vm(2, 51, 16, 128),
+        vm(2, 51, 16, 128),
         vm(4, T2, 48, 128),
         vm(6, T2, 8, 128),
         vm(3, 6, T2, 8, 128),
@@ -575,8 +671,10 @@
         [vm(ROWS[l] + 2, T2, 8, 128) for l in levels],
         [vm(102 if l == 3 else 100, ST_ROWS[l], 128) for l in levels],
         [vm(102 if l == 3 else 100, LIN[l], 128) for l in levels],
+        [vm(2, 102 if l == 3 else 100, 8, 128) for l in levels],
         [vm(T2, ST_ROWS[l], 128) for l in levels],
         [vm(T2, LIN[l], 128) for l in levels],
+        [vm(2, T2, 8, 128) for l in levels],
         [vm(T2, ES_ROWS[l], 128) for l in levels],
         [vm(T2, LIN[l], 128) for l in levels],
         [vm(T2, 8 * ROWS[l], 128) for l in levels],
@@ -591,8 +689,8 @@
         vm(2, ARR, 256),
         vm(16, NAGG),
         vm(T2, 48, 128),
-        pltpu.SemaphoreType.DMA((64,)),
-        pltpu.SemaphoreType.DMA((64,)),
+        pltpu.SemaphoreType.DMA((80,)),
+        pltpu.SemaphoreType.DMA((80,)),
     ]
     vmem = pl.BlockSpec(memory_space=pltpu.VMEM)
     smem = pl.BlockSpec(memory_space=pltpu.SMEM)

time: 269 us -> 198 us (0.74)
  Pallas kernels: 265 us -> 194 us
    pallas_call x1, Pallas kernels: 265 us -> 194 us  [on_device(): pl.pallas_call(functools.partial(kernel, gxn, gyn), out_shape=(out, out),...]
where the time goes in v2:
time: 198 us; the launch traced here: 197 us
  Pallas kernels  194 us (98%)
  local copies, waits for them, and re-layouts  2.3 us (1%)
    pallas_call x1, Pallas kernels, on_device(): pl.pallas_call(functools.partial(kernel, gxn, gyn), out_shape=(out, out),...  194 us

profile of v2, /device:TPU:1, one launch (start us, length us, event | category | flops | bytes accessed | tf_op | source)
XLA Modules:
  0.0 197.4 jit_solution(16973329064705829338)
XLA Ops:
  0.6 194.4 %shard_map.95 = (f32[10,32,128]{2,1,0:T(8,128)}, f32[10,32,128]{2,1,0:T(8,128)}) custom-call(f32[10,32,128]{2,1,0:T(8,128)} %perm.1, f32[10,32,128]{2,1,0:T(8,128)} %stor.1, s32[32,128]{1,0:T(8,128)} %act.1, s32[10,32,128]{2,1,0:T(8,128)} %colour.1, f32[10,32,128]{2,1,0:T(8,128)} %rweight.1, s32[4]{0:T(128)} %sweeps.1, s32[4,128]{1,0:T(4,128)} %amap.1, ...), custom_call_target="tpu_custom_call" | custom-call | tf_op jit(solution)/shard_map/pallas_call | solution.py:698
  195.1 0.0 copy-start
  195.1 1.6 copy.12
  196.7 0.0 copy-done
  196.7 0.7 copy.13
Async XLA Ops:
  195.1 1.6 copy-start

commit v3 on v2

--- a/solution.py
+++ b/solution.py
@@ -17,7 +17,7 @@
 OWN = (32, 16, 8, 4)
 LIN = (48, 48, 40, 32)
 LO = (8, 16, 16, 12)
-WS = (0, 0, 4, 0)
+WS = (8, 0, 4, 0)
 NEAR = (
     (),
     ((1, 8, 16, 8, 16), (-1, 0, 8, 32, 40)),
@@ -44,9 +44,9 @@
 ARR = 24
 ZC = 2
 
-X_PARTNERS = ((1, 0), (2, 0), (3, 0))
+X_PARTNERS = ((1, 0), (2, 0), (3, 0), (0, 1), (1, 1), (2, 1), (3, 1))
 Y_PARTNERS = ((8, 0), (16, 0), (24, 0))
-Z_PARTNERS = ((4, 0), (0, 2), (4, 2))
+Z_PARTNERS = ((4, 0), (0, 2), (4, 2), (0, 1), (4, 1), (0, 3), (4, 3))
 
 
 def pads(buf, rows):
@@ -99,12 +99,13 @@
     source,
     sol,
     fres,
-    y0,
     yp,
-    yn,
-    f0,
+    pw,
+    fc,
+    fh,
     rw,
     raw,
+    p8,
     cfs,
     ccs,
     cis,
@@ -115,6 +116,7 @@
     ks,
     kw,
     kf,
+    kfw,
     sts,
     lrs,
     lrf,
@@ -126,10 +128,8 @@
     agg,
     ar_keep,
     ar_give,
-    ar_core,
     ar_sum,
     ar_in,
-    ar_last,
     ratio,
     wlin,
     send,
@@ -165,143 +165,203 @@
             c.wait()
 
     barrier = pltpu.get_barrier_semaphore()
-    partners = [ring(d, 0) for d in (1, -1, 2, -2, 3, -3)] + [ring(0, 1), ring(0, -1)]
-    partners += [flip(*p) for p in X_PARTNERS + Y_PARTNERS + Z_PARTNERS + ((0, 1),)]
+    partners = [ring(d, 0) for d in (1, -1, 2, -2, 3, -3)] + [ring(dx, dy) for dx in (-1, 0, 1) for dy in (-1, 1)]
+    partners += [flip(*p) for p in X_PARTNERS + Y_PARTNERS + Z_PARTNERS]
     for device in partners:
         pl.semaphore_signal(barrier, inc=1, device_id=device, device_id_type=MESH)
 
+    lane = lax.broadcasted_iota(jnp.int32, (NZ, 8, 128), 2)
+    sub = lax.broadcasted_iota(jnp.int32, (NZ, 8, 128), 1)
+    layer = lax.broadcasted_iota(jnp.int32, (NZ, 8, 128), 0)
+
+    def pack(k, value):
+        part = slice(k * NZ, k * NZ + NZ)
+        for h in (0, 1):
+            v0, v1 = value[:, 16 * h : 16 * h + 8], value[:, 16 * h + 8 : 16 * h + 16]
+            a = jnp.where(sub < 4, v0, pltpu.roll(v1, 4, 1))
+            b = jnp.where(sub < 4, pltpu.roll(v0, 4, 1), v1)
+            rows = slice(8 * h, 8 * h + 8)
+            yp[0, part, rows] = jnp.where(lane < 64, pltpu.roll(a, 64, 2), b)
+            yp[1, part, rows] = jnp.where(lane < 64, a, pltpu.roll(b, 64, 2))
+
+    def unpack(k, h, dst, at, to):
+        part = slice(k * NZ, k * NZ + NZ)
+        left, right = pw[0, part, 8 * h : 8 * h + 8], pw[1, part, 8 * h : 8 * h + 8]
+        a = jnp.where(lane < 64, right, pltpu.roll(left, 64, 2))
+        b = jnp.where(lane < 64, pltpu.roll(right, 64, 2), left)
+        dst[to, at : at + 8] = jnp.where(sub < 4, a, pltpu.roll(b, 4, 1))
+        dst[to, at + 8 : at + 16] = jnp.where(sub < 4, pltpu.roll(a, 4, 1), b)
+
     active = act[...] > 0
     for z in range(NZ):
-        y0[z] = jnp.where(active, perm[z], 0.0)
-        y0[NZ + z] = jnp.where(active, stor[z], 1.0)
-        y0[2 * NZ + z] = colour[z].astype(F32)
-        y0[3 * NZ + z] = source[z]
-        y0[4 * NZ + z] = rweight[z]
+        fc[z, 16:48] = jnp.where(active, perm[z], 0.0)
+        fc[NZ + z, 16:48] = jnp.where(active, stor[z], 1.0)
+        fc[2 * NZ + z, 16:48] = colour[z].astype(F32)
+        fc[3 * NZ + z, 16:48] = source[z]
+    for k in range(4):
+        pack(k, fc[k * NZ : k * NZ + NZ, 16:48])
+    pack(4, rweight[...])
     own_map = amap[...].astype(F32)
-
-    s_y = sems(2)
-    s_x = sems(2)
-
-    lane10 = lax.broadcasted_iota(jnp.int32, (NZ, 16, 128), 2)
-
-    def pack(k):
-        part = slice(k * NZ, k * NZ + NZ)
-        upper, lower = y0[part, 0:16], y0[part, 16:32]
-        yp[0, part] = jnp.where(lane10 < 64, pltpu.roll(upper, 64, 2), lower)
-        yp[1, part] = jnp.where(lane10 < 64, upper, pltpu.roll(lower, 64, 2))
-
-    def y_exchange(span, between):
-        right = copy(yp.at[0, span], yn.at[0, span], s_y, ring(0, 1))
-        left = copy(yp.at[1, span], yn.at[1, span], s_y + 1, ring(0, -1))
+    yp[0, 50, 0:4] = own_map
+    yp[1, 50, 0:4] = own_map
+
+    RAW, RHS = slice(0, 30), slice(30, 40)
+    s_y, s_xr, s_xs, s_cr, s_cs = sems(2), sems(2), sems(2), sems(4), sems(4)
+
+    def beside_copies(v, span, raw_too):
+        dy = 1 - 2 * v
+        out = [copy(yp.at[v, span], pw.at[v, span, 8:24], s_y + v, ring(0, dy))]
+        for q, (dx, a, to) in enumerate(((1, 12, 4), (-1, 0, 24))):
+            out.append(
+                copy(
+                    yp.at[v, RHS, a : a + 4], pw.at[v, RHS, to : to + 4],
+                    s_cs + 2 * v + q, ring(dx, dy),
+                )
+            )
+        if raw_too:
+            for q, (dx, a, to) in enumerate(((1, 8, 0), (-1, 0, 24))):
+                out.append(
+                    copy(
+                        yp.at[v, RAW, a : a + 8], pw.at[v, RAW, to : to + 8],
+                        s_cr + 2 * v + q, ring(dx, dy),
+                    )
+                )
+        return out
+
+    def exchange(span, raw_too, between):
+        along = [
+            copy(fc.at[RHS, 40:48], fc.at[RHS, 8:16], s_xs, ring(1, 0)),
+            copy(fc.at[RHS, 16:24], fc.at[RHS, 48:56], s_xs + 1, ring(-1, 0)),
+        ]
+        if raw_too:
+            along = [
+                copy(fc.at[RAW, 32:48], fc.at[RAW, 0:16], s_xr, ring(1, 0)),
+                copy(fc.at[RAW, 16:32], fc.at[RAW, 48:64], s_xr + 1, ring(-1, 0)),
+            ] + along
+        up, down = beside_copies(0, span, raw_too), beside_copies(1, span, raw_too)
+        start(along)
 
         @pl.when(gy < gyn - 1)
         def _():
-            right.start()
+            start(up)
 
         @pl.when(gy > 0)
         def _():
-            left.start()
-
-        @pl.when(gy == 0)
-        def _():
-            yn[0, span] = yp[0, span]
-
-        @pl.when(gy == gyn - 1)
-        def _():
-            yn[1, span] = yp[1, span]
+            start(down)
+
+        for v, edge in ((0, gy == 0), (1, gy == gyn - 1)):
+
+            @pl.when(edge)
+            def _():
+                pw[v, span, 8:24] = yp[v, span]
+                parts = (RAW, RHS) if raw_too else (RHS,)
+                for part in parts:
+                    pw[v, part, 0:8] = yp[v, part, 8:16]
+                    pw[v, part, 24:32] = yp[v, part, 0:8]
 
         between()
+        finish(along)
 
         @pl.when(gy < gyn - 1)
         def _():
-            right.wait_send()
-            left.wait_recv()
+            for c in up:
+                c.wait_send()
+            for c in down:
+                c.wait_recv()
 
         @pl.when(gy > 0)
         def _():
-            left.wait_send()
-            right.wait_recv()
-
-    def x_copies(span, buf, base):
-        return [
-            copy(buf.at[span, :, 32:40], buf.at[span, :, 0:8], base, ring(1, 0)),
-            copy(buf.at[span, :, 8:16], buf.at[span, :, 40:48], base + 1, ring(-1, 0)),
-        ]
-
-    def join(k):
-        part = slice(k * NZ, k * NZ + NZ)
-        right, left = yn[1, part], yn[0, part]
-        upper = jnp.where(lane10 < 64, right, pltpu.roll(left, 64, 2))
-        lower = jnp.where(lane10 < 64, pltpu.roll(right, 64, 2), left)
-        return upper, lower
-
-    def fill_beside():
+            for c in down:
+                c.wait_send()
+            for c in up:
+                c.wait_recv()
+
+    def fill():
         for j in range(4):
             agg_id = lax.broadcasted_iota(jnp.int32, (NAGG, 128), 0)
             onehot[j] = (agg_id == amap[j : j + 1, :]).astype(jnp.bfloat16)
         agg[...] = jnp.zeros_like(agg)
         wlin[...] = jnp.zeros_like(wlin)
-        for l in (1, 2, 3):
-            lrs[l][...] = jnp.zeros_like(lrs[l])
-            els[l][...] = jnp.zeros_like(els[l])
-        for _, _, _, at, end in FAR[1] + ((0, 0, 0, 0, 4), (0, 0, 0, 44, 48)):
+        for at, end in ((0, 8), (40, 48)):
             kw[1][:, at:end] = jnp.ones((100, end - at, 128), F32)
         for l in (2, 3):
             for _, _, _, at, end in FAR[l]:
                 kw[l][0:100, at:end] = jnp.ones((100, end - at, 128), F32)
         for _, _, _, at, end in FAR[3]:
             kw[3][100:102, at:end] = jnp.zeros((2, end - at, 128), F32)
-        for k in range(4):
-            f0[k, 0:NZ, 8:40] = y0[k * NZ : k * NZ + NZ]
-        wlin[0:NZ, 8:40] = y0[4 * NZ : 5 * NZ]
-
-    for k in range(5):
-        pack(k)
-    yp[0, 50, 0:4] = own_map
-    yp[1, 50, 0:4] = own_map
+        wlin[0:NZ, 8:40] = rweight[...]
+        for i in range(6):
+            rw[i, 0:NZ] = wlin[0:NZ, pl.ds(i, 8, stride=6), :]
+
+    for l in (1, 2, 3):
+        lrs[l][...] = jnp.zeros_like(lrs[l])
+        els[l][...] = jnp.zeros_like(els[l])
     pl.semaphore_wait(barrier, len(partners))
-    y_exchange(slice(0, 51), fill_beside)
+    exchange(slice(0, 51), True, fill)
     for k in range(4):
-        upper, lower = join(k)
-        f0[k, NZ:T2, 8:24] = upper
-        f0[k, NZ:T2, 24:40] = lower
-    upper, lower = join(4)
-    wlin[NZ:T2, 8:24] = upper
-    wlin[NZ:T2, 24:40] = lower
-    start(x_copies(slice(0, 4), f0, s_x))
+        for h in range(4):
+            unpack(k, h, fh, 16 * h, slice(k * NZ, k * NZ + NZ))
+    for h in (1, 2):
+        unpack(4, h, wlin, 16 * h - 8, slice(NZ, T2))
     for i in range(6):
-        rw[i] = wlin[:, pl.ds(i, 8, stride=6), :]
+        rw[i, NZ:T2] = wlin[NZ:T2, pl.ds(i, 8, stride=6), :]
     mlane = lax.broadcasted_iota(jnp.int32, (4, 128), 1)
     ks[3][100, 8:12] = own_map
-    ks[3][101, 8:12] = jnp.where(mlane < 64, yn[1, 50, 0:4], yn[0, 50, 0:4])
-    finish(x_copies(slice(0, 4), f0, s_x))
-
-    ea0 = eas[0]
-    for i in range(6):
-        ea0[i + 1] = f0[0, :, pl.ds(i, 8, stride=6), :]
-    pads(ea0, 6)
-    lane = lax.broadcasted_iota(jnp.int32, (NZ, 8, 128), 2)
-    sub = lax.broadcasted_iota(jnp.int32, (NZ, 8, 128), 1)
-    layer = lax.broadcasted_iota(jnp.int32, (NZ, 8, 128), 0)
+    ks[3][101, 8:12] = jnp.where(mlane < 64, pw[1, 50, 8:12], pw[0, 50, 8:12])
+
+    def raw_rows(k, at, stride):
+        part = slice(k * NZ, k * NZ + NZ)
+        rows = pl.ds(at, 8, stride=stride)
+        return jnp.concatenate([fc[part, rows, :], fh[part, rows, :]], axis=0)
+
+    for i in range(8):
+        p8[i + 1] = raw_rows(0, i, 8)
+    pads(p8, 8)
 
     def harmonic(a, b):
         total = a + b
         return jnp.where(total > 0, 2.0 * a * b / jnp.where(total > 0, total, 1.0), 0.0)
 
-    for i in range(6):
-        own = [ea0[i + 1, t * NZ : t * NZ + NZ] for t in (0, 1)]
-        north = beside(own[0], own[1], 127, lane == 127)
-        xg = gx * 32 - 8 + 6 * sub + i
-        for t in (0, 1):
-            part = slice(t * NZ, t * NZ + NZ)
-            west = harmonic(own[t], ea0[i, part])
-            yg = gy * 128 + lane
-            if t == 1:
-                yg = jnp.where(lane < 64, yg + 128, yg - 128)
-            raw[0, i, part] = jnp.where((xg == 0) | (xg == 1024), 0.0, west)
-            raw[1, i, part] = jnp.where(jnp.bitwise_and(yg, 511) == 511, 0.0, harmonic(own[t], north[t]))
-            above = 0.5 * harmonic(own[t], zshift(ea0, i + 1, own[t], t, 0, NZ, True))
-            raw[2, i, part] = jnp.where(layer == NZ - 1, 0.0, above)
+    for m in range(4):
+        pair = []
+        for i in (2 * m, 2 * m + 1):
+            own = [p8[i + 1, t * NZ : t * NZ + NZ] for t in (0, 1)]
+            north = beside(own[0], own[1], 127, lane == 127)
+            xg = gx * 32 - 16 + 8 * sub + i
+            three = [[], [], []]
+            for t in (0, 1):
+                part = slice(t * NZ, t * NZ + NZ)
+                yg = gy * 128 + lane
+                if t == 1:
+                    yg = jnp.where(lane < 64, yg + 128, yg - 128)
+                west = harmonic(own[t], p8[i, part])
+                above = 0.5 * harmonic(own[t], zshift(p8, i + 1, own[t], t, 0, NZ, True))
+                three[0].append(jnp.where((xg == 0) | (xg == 1024), 0.0, west))
+                three[1].append(
+                    jnp.where(jnp.bitwise_and(yg, 511) == 511, 0.0, harmonic(own[t], north[t]))
+                )
+                three[2].append(jnp.where(layer == NZ - 1, 0.0, above))
+            three = [jnp.concatenate(f, axis=0) for f in three]
+            for k in range(3):
+                raw[k, :, pl.ds(i, 8, stride=8), :] = three[k]
+            pair.append(three)
+        five = (
+            raw_rows(1, 2 * m, 8) + raw_rows(1, 2 * m + 1, 8),
+            pair[0][0],
+            pair[0][1] + pair[1][1],
+            pair[0][2] + pair[1][2],
+            raw_rows(2, 2 * m, 8),
+        )
+        for k in range(5):
+            kw[1][k * T2 : k * T2 + T2, pl.ds(8 + m, 8, stride=4), :] = five[k]
+
+    for l, finer, at in ((2, kw[1], 16), (3, ks[2], 8)):
+        for k in range(5):
+            part = slice(k * T2, k * T2 + T2)
+            value = finer[part, pl.ds(at, 8, stride=2), :]
+            if k not in (1, 4):
+                value = value + finer[part, pl.ds(at + 1, 8, stride=2), :]
+            ks[l][part, 8:16] = value
 
     def scaled(l, storage_of, west_of, north_of, above_of, colour_of):
         rows, pad = ROWS[l], eas[l]
@@ -328,36 +388,19 @@
                 cis[l][i, part] = inverse
                 cols[l][i, part] = shade[part]
 
-    def pick0(k):
-        return lambda i: f0[k, :, pl.ds(i, 8, stride=6), :]
-
-    scaled(0, pick0(1), lambda i: raw[0, i], lambda i: raw[1, i], lambda i: raw[2, i], pick0(2))
-
-    for m in range(3):
-        even, odd = 2 * m, 2 * m + 1
-        five = (
-            f0[1, :, pl.ds(even, 8, stride=6), :] + f0[1, :, pl.ds(odd, 8, stride=6), :],
-            raw[0, even],
-            raw[1, even] + raw[1, odd],
-            raw[2, even] + raw[2, odd],
-            f0[2, :, pl.ds(even, 8, stride=6), :],
-        )
-        for k in range(5):
-            ks[1][k * T2 : k * T2 + T2, pl.ds(4 + m, 8, stride=3), :] = five[k]
-    for l in (2, 3):
-        for k in range(5):
-            part = slice(k * T2, k * T2 + T2)
-            value = ks[l - 1][part, pl.ds(8, 8, stride=2), :]
-            if k not in (1, 4):
-                value = value + ks[l - 1][part, pl.ds(9, 8, stride=2), :]
-            ks[l][part, 8:16] = value
+    def face0(k):
+        return lambda i: raw[k, :, pl.ds(WS[0] + i, 8, stride=6), :]
+
+    def raw0(k):
+        return lambda i: raw_rows(k, WS[0] + i, 6)
 
     s_kn = [sems(len(NEAR[l])) for l in range(4)]
     s_kf = [sems(len(FAR[l])) for l in range(4)]
     s_rn = [sems(len(NEAR[l])) for l in range(4)]
     s_rf = [sems(len(FAR[l])) for l in range(4)]
     s_e = [sems(len(ITERATE[l])) for l in range(4)]
-    s_ar = sems(22)
+    s_ar = sems(34)
+    s_kw = sems(1)
 
     def near_copies(l, src, own_at, dst, base, table):
         return [
@@ -365,10 +408,10 @@
             for k, (right, a, b, c, d) in enumerate(table)
         ]
 
-    def far_copies(l, src, dst, base):
+    def far_copies(l, src, own_at, dst, base):
         return [
             copy(
-                src.at[:, SO + a : SO + b], dst.at[k, :, c % 8 : c % 8 + 4], base + k, ring(right, 0)
+                src.at[:, own_at + a : own_at + b], dst.at[k, :, c % 8 : c % 8 + 4], base + k, ring(right, 0)
             )
             for k, (right, a, b, c, d) in enumerate(FAR[l])
         ]
@@ -387,10 +430,15 @@
         return near_copies(l, ks[l], SO, kw[l], s_kn[l], NEAR[l])
 
     def kf_copies(l):
-        return far_copies(l, ks[l], kf[l], s_kf[l])
+        if l > 1:
+            return far_copies(l, ks[l], SO, kf[l], s_kf[l])
+        west = slice(T2, 2 * T2)
+        return far_copies(1, kw[1], LO[1], kf[1], s_kf[1]) + [
+            copy(kw[1].at[west, 24:28], kfw.at[:, 0:4], s_kw, ring(1, 0))
+        ]
 
     def rf_copies(l):
-        return far_copies(l, sts[l], lrf[l], s_rf[l])
+        return far_copies(l, sts[l], SO, lrf[l], s_rf[l])
 
     def level_coefficients(l):
         def pick(k):
@@ -415,10 +463,13 @@
             ccs[l][i, span[t]] * (rps[l][i, span[t]] + sums[t] - own[t]) for t in (0, 1)
         ]
 
-    def before(l, lin):
+    def before(l):
         ea, eb = eas[l], ebs[l]
         for i in range(ROWS[l]):
-            scaled_rhs = lin[:, pl.ds(WS[l] + i, 8, stride=ROWS[l]), :] * cis[l][i]
+            if l == 0:
+                scaled_rhs = raw_rows(3, WS[0] + i, 6) * cis[0][i]
+            else:
+                scaled_rhs = lrs[l][:, pl.ds(WS[l] + i, 8, stride=ROWS[l]), :] * cis[l][i]
             rps[l][i] = scaled_rhs
             ea[i + 1] = jnp.where(cols[l][i] == 0.0, scaled_rhs, 0.0)
         pads(ea, ROWS[l])
@@ -468,7 +519,7 @@
         return near_copies(l, ess[l], ES_OFF[l] + HALO[l], els[l], s_e[l], ITERATE[l])
 
     def aggregate_ratio(cyc):
-        s_a = s_ar + cyc * 11
+        s_a = s_ar + cyc * 17
         for first in range(0, NZ, ZC):
             for i in range(4):
                 span, res = left_over(3, ebs[3], i, first, first + ZC)
@@ -493,28 +544,38 @@
         low_half, high_half = mine[:, 0:256], mine[:, 256:512]
         ar_keep[...] = jnp.where(core == 0, low_half, high_half)
         ar_give[...] = jnp.where(core == 0, high_half, low_half)
-        first_copy = copy(ar_give, ar_core.at[cyc], s_a, flip(0, 1))
-        first_copy.start()
         stage_iterate(3)
-        first_copy.wait()
-        ar_sum[0] = ar_keep[...] + ar_core[cyc]
-        at = 1
+        at = s_a
         for stage, group in enumerate((X_PARTNERS, Y_PARTNERS, Z_PARTNERS)):
-            copies = [
-                copy(ar_sum.at[stage], ar_in.at[cyc, stage, k], s_a + at + k, flip(*p))
-                for k, p in enumerate(group)
-            ]
+            copies = []
+            for k, p in enumerate(group):
+                src = ar_sum.at[stage]
+                if stage == 0:
+                    src = ar_give if p[1] else ar_keep
+                copies.append(copy(src, ar_in.at[cyc, stage, k], at + k, flip(*p)))
+            at += len(group)
             start(copies)
             if stage == 0:
-                start(e_copies(3))
+                start(e_copies(3) + e_copies(2) + rf_copies(2))
+
+                @pl.when(cyc == 0)
+                def _():
+                    start(kf_copies(2))
+
                 keep_own(3, ess[3], 16, els[3])
+            if stage == 2:
+
+                @pl.when(cyc == 0)
+                def _():
+                    start(kf_copies(1))
+
             finish(copies)
-            ar_sum[stage + 1] = ar_sum[stage] + ar_in[cyc, stage, 0] + ar_in[cyc, stage, 1] + ar_in[cyc, stage, 2]
-            at += 3
-        last_copy = copy(ar_sum.at[3], ar_last.at[cyc], s_a + 10, flip(0, 1))
-        last_copy.start()
-        last_copy.wait()
-        mine, other = ar_sum[3], ar_last[cyc]
+            mine = ar_keep[...] if stage == 0 else ar_sum[stage]
+            for k in range(7 if stage == 0 else 3):
+                mine = mine + ar_in[cyc, stage, k]
+            if stage < 2:
+                ar_sum[stage + 1] = mine
+        other = ar_in[cyc, 2, 3] + ar_in[cyc, 2, 4] + ar_in[cyc, 2, 5] + ar_in[cyc, 2, 6]
         low_half = jnp.where(core == 0, mine, other)
         high_half = jnp.where(core == 0, other, mine)
         ratio[0:NZ, 0:256] = low_half[0:NZ] / low_half[NZ:T2]
@@ -527,6 +588,8 @@
             def _():
                 finish(kf_copies(l))
                 merge_far(l, kf[l], kw[l])
+                if l == 1:
+                    kw[1][T2 : 2 * T2, 8:12] = kfw[:, 0:4]
                 level_coefficients(l)
 
             finish(rf_copies(l))
@@ -535,7 +598,8 @@
                 rps[l][i] = lrs[l][:, pl.ds(WS[l] + i, 8, stride=ROWS[l]), :] * cis[l][i]
         finish(e_copies(l))
         for i in range(ROWS[l]):
-            now = els[l][:, pl.ds(WS[l] + i, 8, stride=ROWS[l]), :]
+            at = 0 if l == 0 else WS[l]
+            now = els[l][:, pl.ds(at + i, 8, stride=ROWS[l]), :]
             if l < 3:
                 at = HALO[l + 1] - HALO[l] // 2 + i // 2
                 now = now + cls[l + 1][:, pl.ds(at, 8, stride=ROWS[l] // 2), :]
@@ -559,32 +623,33 @@
 
         lax.fori_loop(0, 4, row, 0)
 
-    for l in (1, 2, 3):
-        start(kn_copies(l))
+    start(kn_copies(2))
+    scaled(0, raw0(1), face0(0), face0(1), face0(2), raw0(2))
 
     def cycle(cyc, carry):
         first = cyc == 0
         for l in range(4):
-            before(l, f0.at[3] if l == 0 else lrs[l])
+            before(l)
             if l < 3:
                 restrict(l)
                 start(rn_copies(l + 1))
+
+                @pl.when(first)
+                def _():
+                    start(kn_copies(3) if l == 0 else kf_copies(3) if l == 2 else [])
+
                 stage_iterate(l)
-                if l > 0:
-                    start(rf_copies(l))
-                start(e_copies(l))
-                if l == 2:
-                    start(rf_copies(3))
+                if l == 1:
+                    start(rf_copies(1))
+                start(e_copies(l) if l < 2 else rf_copies(3))
                 keep_own(l, ess[l], ES_OFF[l] + HALO[l], els[l])
                 keep_own(l + 1, sts[l + 1], SO, lrs[l + 1])
 
                 @pl.when(first)
                 def _():
-                    if l == 2:
-                        for k in (3, 2, 1):
-                            start(kf_copies(k))
-                    keep_own(l + 1, ks[l + 1], SO, kw[l + 1])
-                    finish(kn_copies(l + 1))
+                    if l > 0:
+                        keep_own(l + 1, ks[l + 1], SO, kw[l + 1])
+                        finish(kn_copies(l + 1))
                     level_coefficients(l + 1)
 
                 finish(rn_copies(l + 1))
@@ -608,42 +673,32 @@
                     cls[l][:, pl.ds(i, 8, stride=ROWS[l]), :] = eas[l][i + 1]
 
         for i in range(6):
-            wlin[0:NZ, pl.ds(i, 8, stride=6), :] = eas[0][i + 1, 0:NZ]
-        added = wlin[0:NZ, 8:40]
-
-        @pl.when(first)
-        def _():
-            sol[...] = added
-
-        @pl.when(jnp.logical_not(first))
-        def _():
-            sol[...] += added
-
-        for i in range(6):
             for z in range(0, NZ, ZC):
                 span, res = left_over(0, eas[0], i, z, z + ZC)
                 wlin[span[0], pl.ds(i, 8, stride=6), :] = res[0]
         leftover = wlin[0:NZ, 8:40]
 
+        def result():
+            for i in range(6):
+                wlin[0:NZ, pl.ds(i, 8, stride=6), :] = eas[0][i + 1, 0:NZ]
+            return wlin[0:NZ, 8:40]
+
         @pl.when(first)
         def _():
-            part = slice(3 * NZ, 4 * NZ)
-            y0[part] = leftover
-            pack(3)
-
-            def fill_own():
-                f0[3, 0:NZ, 8:40] = y0[part]
-
-            y_exchange(part, fill_own)
-            upper, lower = join(3)
-            f0[3, NZ:T2, 8:24] = upper
-            f0[3, NZ:T2, 24:40] = lower
-            start(x_copies(slice(3, 4), f0, s_x))
-            finish(x_copies(slice(3, 4), f0, s_x))
+            fc[RHS, 16:48] = leftover
+            pack(3, leftover)
+
+            def keep():
+                sol[...] = result()
+
+            exchange(RHS, False, keep)
+            for h in range(4):
+                unpack(3, h, fh, 16 * h, RHS)
 
         @pl.when(jnp.logical_not(first))
         def _():
             fres[...] = leftover
+            sol[...] += result()
 
         return carry
 
@@ -656,12 +711,13 @@
 
     levels = range(LEVELS)
     scratch = [
-        vm(50, 32, 128),
         vm(2, 51, 16, 128),
-        vm(2, 51, 16, 128),
-        vm(4, T2, 48, 128),
+        vm(2, 51, 32, 128),
+        vm(40, 64, 128),
+        vm(40, 64, 128),
         vm(6, T2, 8, 128),
-        vm(3, 6, T2, 8, 128),
+        vm(3, T2, 64, 128),
+        vm(10, T2, 8, 128),
         [vm(ROWS[l], 6, T2, 8, 128) for l in levels],
         [vm(ROWS[l], T2, 8, 128) for l in levels],
         [vm(ROWS[l], T2, 8, 128) for l in levels],
@@ -672,6 +728,7 @@
         [vm(102 if l == 3 else 100, ST_ROWS[l], 128) for l in levels],
         [vm(102 if l == 3 else 100, LIN[l], 128) for l in levels],
         [vm(2, 102 if l == 3 else 100, 8, 128) for l in levels],
+        vm(T2, 8, 128),
         [vm(T2, ST_ROWS[l], 128) for l in levels],
         [vm(T2, LIN[l], 128) for l in levels],
         [vm(2, T2, 8, 128) for l in levels],
@@ -683,14 +740,12 @@
         vm(ARR, 128),
         vm(ARR, 256),
         vm(ARR, 256),
-        vm(2, ARR, 256),
         vm(4, ARR, 256),
-        vm(2, 3, 3, ARR, 256),
-        vm(2, ARR, 256),
+        vm(2, 3, 7, ARR, 256),
         vm(16, NAGG),
         vm(T2, 48, 128),
-        pltpu.SemaphoreType.DMA((80,)),
-        pltpu.SemaphoreType.DMA((80,)),
+        pltpu.SemaphoreType.DMA((112,)),
+        pltpu.SemaphoreType.DMA((112,)),
     ]
     vmem = pl.BlockSpec(memory_space=pltpu.VMEM)
     smem = pl.BlockSpec(memory_space=pltpu.SMEM)

time: 198 us -> 168 us (0.85)
  Pallas kernels: 194 us -> 165 us
    pallas_call x1, Pallas kernels: 194 us -> 165 us  [on_device(): pl.pallas_call(functools.partial(kernel, gxn, gyn), out_shape=(out, out),...]
where the time goes in v3:
time: 168 us
  Pallas kernels  165 us (98%)
  local copies, waits for them, and re-layouts  2.3 us (1%)
    pallas_call x1, Pallas kernels, on_device(): pl.pallas_call(functools.partial(kernel, gxn, gyn), out_shape=(out, out),...  165 us

profile of v3, /device:TPU:1, one launch (start us, length us, event | category | flops | bytes accessed | tf_op | source)
XLA Modules:
  0.0 168.1 jit_solution(16507341340731642468)
XLA Ops:
  0.6 165.2 %shard_map.95 = (f32[10,32,128]{2,1,0:T(8,128)}, f32[10,32,128]{2,1,0:T(8,128)}) custom-call(f32[10,32,128]{2,1,0:T(8,128)} %perm.1, f32[10,32,128]{2,1,0:T(8,128)} %stor.1, s32[32,128]{1,0:T(8,128)} %act.1, s32[10,32,128]{2,1,0:T(8,128)} %colour.1, f32[10,32,128]{2,1,0:T(8,128)} %rweight.1, s32[4]{0:T(128)} %sweeps.1, s32[4,128]{1,0:T(4,128)} %amap.1, ...), custom_call_target="tpu_custom_call" | custom-call | tf_op jit(solution)/shard_map/pallas_call | solution.py:753
  165.8 0.0 copy-start
  165.8 1.6 copy.12
  167.5 0.0 copy-done
  167.5 0.7 copy.13
Async XLA Ops:
  165.8 1.6 copy-start

commit v4 on v3

--- a/solution.py
+++ b/solution.py
@@ -89,16 +89,23 @@
 def kernel(
     gxn,
     gyn,
+    perm_hbm,
+    stor_hbm,
+    act_hbm,
+    colour_hbm,
+    rweight_hbm,
+    sweeps,
+    amap,
+    source_hbm,
+    sol,
+    fres,
     perm,
     stor,
     act,
     colour,
     rweight,
-    sweeps,
-    amap,
     source,
-    sol,
-    fres,
+    load,
     yp,
     pw,
     fc,
@@ -170,6 +177,20 @@
     for device in partners:
         pl.semaphore_signal(barrier, inc=1, device_id=device, device_id_type=MESH)
 
+    loads = [
+        pltpu.make_async_copy(there, here, load.at[k])
+        for k, (there, here) in enumerate(
+            (
+                (perm_hbm, perm), (stor_hbm, stor), (act_hbm, act), (colour_hbm, colour),
+                (rweight_hbm, rweight), (source_hbm, source),
+            )
+        )
+    ]
+    start(loads)
+    for l in (1, 2, 3):
+        lrs[l][...] = jnp.zeros_like(lrs[l])
+        els[l][...] = jnp.zeros_like(els[l])
+    finish(loads)
     lane = lax.broadcasted_iota(jnp.int32, (NZ, 8, 128), 2)
     sub = lax.broadcasted_iota(jnp.int32, (NZ, 8, 128), 1)
     layer = lax.broadcasted_iota(jnp.int32, (NZ, 8, 128), 0)
@@ -293,9 +314,6 @@
         for i in range(6):
             rw[i, 0:NZ] = wlin[0:NZ, pl.ds(i, 8, stride=6), :]
 
-    for l in (1, 2, 3):
-        lrs[l][...] = jnp.zeros_like(lrs[l])
-        els[l][...] = jnp.zeros_like(els[l])
     pl.semaphore_wait(barrier, len(partners))
     exchange(slice(0, 51), True, fill)
     for k in range(4):
@@ -355,13 +373,14 @@
         for k in range(5):
             kw[1][k * T2 : k * T2 + T2, pl.ds(8 + m, 8, stride=4), :] = five[k]
 
-    for l, finer, at in ((2, kw[1], 16), (3, ks[2], 8)):
-        for k in range(5):
-            part = slice(k * T2, k * T2 + T2)
-            value = finer[part, pl.ds(at, 8, stride=2), :]
-            if k not in (1, 4):
-                value = value + finer[part, pl.ds(at + 1, 8, stride=2), :]
-            ks[l][part, 8:16] = value
+    def own_coefficients():
+        for l, finer, at in ((2, kw[1], 16), (3, ks[2], 8)):
+            for k in range(5):
+                part = slice(k * T2, k * T2 + T2)
+                value = finer[part, pl.ds(at, 8, stride=2), :]
+                if k not in (1, 4):
+                    value = value + finer[part, pl.ds(at + 1, 8, stride=2), :]
+                ks[l][part, 8:16] = value
 
     def scaled(l, storage_of, west_of, north_of, above_of, colour_of):
         rows, pad = ROWS[l], eas[l]
@@ -427,7 +446,22 @@
             dst[:, 28:32] = src[:, src_at : src_at + n]
 
     def kn_copies(l):
-        return near_copies(l, ks[l], SO, kw[l], s_kn[l], NEAR[l])
+        if l == 2:
+            return near_copies(l, ks[l], SO, kw[l], s_kn[l], NEAR[l])
+        maps, base = slice(100, 102), s_kn[3]
+        return near_copies(l, ks[l], SO, kw[l], base, NEAR[3][2:]) + [
+            copy(ks[3].at[maps, SO : SO + 4], kw[3].at[maps, c:d], base + 2 + k, ring(right, 0))
+            for k, (right, _, _, c, d) in enumerate(NEAR[3][:2])
+        ]
+
+    def nearest_blocks():
+        for k in range(5):
+            part = slice(k * T2, k * T2 + T2)
+            for at, to in ((8, 8), (16, 12)):
+                value = kw[2][part, pl.ds(at, 8, stride=2), :]
+                if k not in (1, 4):
+                    value = value + kw[2][part, pl.ds(at + 1, 8, stride=2), :]
+                kw[3][part, to : to + 8] = value
 
     def kf_copies(l):
         if l > 1:
@@ -623,7 +657,6 @@
 
         lax.fori_loop(0, 4, row, 0)
 
-    start(kn_copies(2))
     scaled(0, raw0(1), face0(0), face0(1), face0(2), raw0(2))
 
     def cycle(cyc, carry):
@@ -636,7 +669,11 @@
 
                 @pl.when(first)
                 def _():
-                    start(kn_copies(3) if l == 0 else kf_copies(3) if l == 2 else [])
+                    if l == 0:
+                        own_coefficients()
+                        start(kn_copies(2) + kn_copies(3))
+                    if l == 2:
+                        start(kf_copies(3))
 
                 stage_iterate(l)
                 if l == 1:
@@ -647,6 +684,8 @@
 
                 @pl.when(first)
                 def _():
+                    if l == 2:
+                        nearest_blocks()
                     if l > 0:
                         keep_own(l + 1, ks[l + 1], SO, kw[l + 1])
                         finish(kn_copies(l + 1))
@@ -710,7 +749,15 @@
         return pltpu.VMEM(shape, dtype)
 
     levels = range(LEVELS)
+    block = perm.shape
     scratch = [
+        vm(*block),
+        vm(*block),
+        vm(*act.shape, dtype=jnp.int32),
+        vm(*block, dtype=jnp.int32),
+        vm(*block),
+        vm(*block),
+        pltpu.SemaphoreType.DMA((6,)),
         vm(2, 51, 16, 128),
         vm(2, 51, 32, 128),
         vm(40, 64, 128),
@@ -749,11 +796,12 @@
     ]
     vmem = pl.BlockSpec(memory_space=pltpu.VMEM)
     smem = pl.BlockSpec(memory_space=pltpu.SMEM)
+    there = pl.BlockSpec(memory_space=pl.ANY)
     out = jax.ShapeDtypeStruct(perm.shape, F32)
     return pl.pallas_call(
         functools.partial(kernel, gxn, gyn),
         out_shape=(out, out),
-        in_specs=[vmem, vmem, vmem, vmem, vmem, smem, vmem, vmem],
+        in_specs=[there, there, there, there, there, smem, vmem, there],
         out_specs=(vmem, vmem),
         scratch_shapes=scratch,
         compiler_params=pltpu.CompilerParams(

time: 168 us -> 164 us (0.976)
  Pallas kernels: 165 us -> 161 us
    pallas_call x1, Pallas kernels: 165 us -> 161 us  [on_device(): pl.pallas_call(functools.partial(kernel, gxn, gyn), out_shape=(out, out),...]
where the time goes in v4:
time: 164 us
  Pallas kernels  161 us (98%)
  local copies, waits for them, and re-layouts  2.3 us (1%)
    pallas_call x1, Pallas kernels, on_device(): pl.pallas_call(functools.partial(kernel, gxn, gyn), out_shape=(out, out),...  161 us

profile of v4, /device:TPU:1, one launch (start us, length us, event | category | flops | bytes accessed | tf_op | source)
XLA Modules:
  0.0 163.9 jit_solution(14513699235013195450)
XLA Ops:
  0.6 160.9 %shard_map.95 = (f32[10,32,128]{2,1,0:T(8,128)}, f32[10,32,128]{2,1,0:T(8,128)}) custom-call(f32[10,32,128]{2,1,0:T(8,128)} %perm_hbm.1, f32[10,32,128]{2,1,0:T(8,128)} %stor_hbm.1, s32[32,128]{1,0:T(8,128)} %act_hbm.1, s32[10,32,128]{2,1,0:T(8,128)} %colour_hbm.1, f32[10,32,128]{2,1,0:T(8,128)} %rweight_hbm.1, s32[4]{0:T(128)} %sweeps.1, s32[4,128]{1,0:T(4,128)} %amap.1, ...), custom_call_target="tpu_custom_call" | custom-call | tf_op jit(solution)/shard_map/pallas_call | solution.py:801
  161.6 0.0 copy-start
  161.6 1.6 copy.12
  163.2 0.0 copy-done
  163.2 0.7 copy.13
Async XLA Ops:
  161.6 1.6 %copy-start = (f32[10,32,128]{2,1,0:T(8,128)S(1)}, f32[10,32,128]{2,1,0:T(8,128)}, u32[]{:S(2)}) copy-start(f32[10,32,128]{2,1,0:T(8,128)} %get-tuple-element.5) | copy-start | bytes 491524

commit v5 on v4

--- a/solution.py
+++ b/solution.py
@@ -381,6 +381,8 @@
                 if k not in (1, 4):
                     value = value + finer[part, pl.ds(at + 1, 8, stride=2), :]
                 ks[l][part, 8:16] = value
+            if l == 2:
+                start(kn_copies(2))
 
     def scaled(l, storage_of, west_of, north_of, above_of, colour_of):
         rows, pad = ROWS[l], eas[l]
@@ -666,19 +668,22 @@
             if l < 3:
                 restrict(l)
                 start(rn_copies(l + 1))
+                if l == 2:
+                    start(rf_copies(3))
 
                 @pl.when(first)
                 def _():
                     if l == 0:
                         own_coefficients()
-                        start(kn_copies(2) + kn_copies(3))
+                        start(kn_copies(3))
                     if l == 2:
                         start(kf_copies(3))
 
                 stage_iterate(l)
                 if l == 1:
                     start(rf_copies(1))
-                start(e_copies(l) if l < 2 else rf_copies(3))
+                if l < 2:
+                    start(e_copies(l))
                 keep_own(l, ess[l], ES_OFF[l] + HALO[l], els[l])
                 keep_own(l + 1, sts[l + 1], SO, lrs[l + 1])
 

time: 164 us -> 164 us (level)
  no operation moved by 1% of the time
where the time goes in v5:
time: 164 us
  Pallas kernels  161 us (98%)
  local copies, waits for them, and re-layouts  2.3 us (1%)
    pallas_call x1, Pallas kernels, on_device(): pl.pallas_call(functools.partial(kernel, gxn, gyn), out_shape=(out, out),...  161 us

profile of v5, /device:TPU:1, one launch (start us, length us, event | category | flops | bytes accessed | tf_op | source)
XLA Modules:
  0.0 163.9 jit_solution(11255344505236022400)
XLA Ops:
  0.6 161.0 %shard_map.95 = (f32[10,32,128]{2,1,0:T(8,128)}, f32[10,32,128]{2,1,0:T(8,128)}) custom-call(f32[10,32,128]{2,1,0:T(8,128)} %perm_hbm.1, f32[10,32,128]{2,1,0:T(8,128)} %stor_hbm.1, s32[32,128]{1,0:T(8,128)} %act_hbm.1, s32[10,32,128]{2,1,0:T(8,128)} %colour_hbm.1, f32[10,32,128]{2,1,0:T(8,128)} %rweight_hbm.1, s32[4]{0:T(128)} %sweeps.1, s32[4,128]{1,0:T(4,128)} %amap.1, ...), custom_call_target="tpu_custom_call" | custom-call | tf_op jit(solution)/shard_map/pallas_call | solution.py:806
  161.6 0.0 copy-start
  161.6 1.6 copy.12
  163.2 0.0 copy-done
  163.2 0.7 copy.13
Async XLA Ops:
  161.6 1.6 %copy-start = (f32[10,32,128]{2,1,0:T(8,128)S(1)}, f32[10,32,128]{2,1,0:T(8,128)}, u32[]{:S(2)}) copy-start(f32[10,32,128]{2,1,0:T(8,128)} %get-tuple-element.5) | copy-start | bytes 491524
